TPU v7x, 256 devices: a whole 4x4x8 slice. The times are simulated.
256 devices in a mesh: ctx: 32 (over y, z_lo, x), exp: 8 (over z_hi, core).
Axes of the slice: x: 4, y: 4, z: 8 (z_hi: 4, z_lo: 2; z = z_hi * 2 + z_lo), core: 2. Of those that a mesh axis runs over, the one named last changes fastest.
Arguments:
- lin_query: bfloat16 [4096, 8192], P('ctx', 'exp'), may hold values from -5 to 5
- lin_key: bfloat16 [4096, 8192], P('ctx', 'exp'), may hold values from -5 to 5
- lin_value: bfloat16 [4096, 8192], P('ctx', 'exp'), may hold values from -5 to 5
- log_decay: float32 [4096, 64], P('ctx', 'exp'), may hold values from -1.5 to 0
- lin_gain: float32 [8192], P('exp'), may hold values from 0.25 to 1.75
- moe_input: bfloat16 [1536, 6144], P(('ctx', 'exp')), may hold values from -6 to 6
- routes: int32 [1536, 2], P(('ctx', 'exp')), may hold values from 0 to 7, all different within a row; in each aligned block of 6 rows (0 to 5, 6 to 11, ...) at most 2 rows name the same one
- route_weight: float32 [1536, 2], P(('ctx', 'exp')), may hold values from 0.2 to 1
- gate_weight: bfloat16 [8, 6144, 9216], P('exp', None, 'ctx'), may hold values from -0.078125 to 0.078125
- up_weight: bfloat16 [8, 6144, 9216], P('exp', None, 'ctx'), may hold values from -0.078125 to 0.078125
- down_weight: bfloat16 [8, 9216, 6144], P('exp', 'ctx'), may hold values from -0.0625 to 0.0625
- soft_query: bfloat16 [4096, 8192], P('ctx', 'exp'), may hold values from -5 to 5
- soft_kv: bfloat16 [4096, 8, 2, 128], P('ctx', 'exp'), may hold values from -5 to 5
Outputs:
- lin_out: bfloat16 [4096, 8192], P('ctx', 'exp')
- moe_out: bfloat16 [1536, 6144], P(('ctx', 'exp'))
- soft_out: bfloat16 [4096, 8192], P('ctx', 'exp')
Inputs may be any that keep to these rules, and one draw needn't show every extreme that they name: `routes`: within the rows of one device (6 rows) each expert is named by at most 2 of them; the 2 experts of a row differ.
All inputs are finite; a program needn't handle non-finite values.
Results may differ from a plain program's by a relative error of at most 0.009.
Values may be sent and summed in bfloat16 or wider, within the bound.
A program may use at most 128 MiB of HBM per device.

v0:
```python
import math

import jax
import jax.numpy as jnp
from jax import lax
from jax.sharding import PartitionSpec as P

D = 6144
HEAD_TOTAL = 64
HEAD = 128
KV_HEADS = 8
EXPERTS = 8
TOP = 2
CAP = 2


def prefix(value, axis, join, neutral):
    count, mine = (lax.axis_size(axis), lax.axis_index(axis))
    pieces = jax.tree.map(lambda part: lax.all_gather(part, axis), value)
    so_far = jax.tree.map(
        lambda part, zero: jnp.full_like(part, 0) + jnp.asarray(zero, part.dtype), value, neutral
    )

    def hop(position, so_far):
        longer = join(so_far, jax.tree.map(lambda part: part[position], pieces))
        return jax.tree.map(lambda new, old: jnp.where(position < mine, new, old), longer, so_far)

    return lax.fori_loop(0, count - 1, hop, so_far)


def lightning(lin_query, lin_key, lin_value, log_decay, lin_gain):
    length = lin_query.shape[0]
    heads_here = log_decay.shape[1]
    score_scale = 1.0 / math.sqrt(HEAD)
    queries = lin_query.reshape(length, heads_here, HEAD)
    key_rows = lin_key.reshape(length, heads_here, HEAD)
    value_f = lin_value.reshape(length, heads_here, HEAD).astype(jnp.float32)
    cumulative = jnp.cumsum(log_decay, axis=0)
    scores = (
        jnp.einsum("thd,jhd->htj", queries, key_rows, preferred_element_type=jnp.float32)
        * score_scale
    )
    spread = cumulative.T[:, :, None] - cumulative.T[:, None, :]
    causal = jnp.tril(jnp.ones((length, length), dtype=jnp.bool_))
    decays = jnp.where(causal[None], jnp.exp(jnp.where(causal[None], spread, 0.0)), 0.0)
    within = jnp.einsum("htj,jhd->thd", scores * decays, value_f, precision=lax.Precision.HIGHEST)
    tail_decay = jnp.exp(cumulative[-1][None, :] - cumulative)
    local_state = jnp.einsum(
        "th,thd,the->hde",
        tail_decay,
        key_rows.astype(jnp.float32),
        value_f,
        precision=lax.Precision.HIGHEST,
    )

    def combine(earlier, latter):
        return (earlier[0] + latter[0], jnp.exp(latter[0])[:, None, None] * earlier[1] + latter[1])

    identity = (
        jnp.zeros((heads_here,), jnp.float32),
        jnp.zeros((heads_here, HEAD, HEAD), jnp.float32),
    )
    prior_log, prior_state = prefix((cumulative[-1], local_state), "ctx", combine, identity)
    carried = (
        jnp.exp(cumulative)[:, :, None]
        * jnp.einsum(
            "thd,hde->the",
            queries.astype(jnp.float32),
            prior_state,
            precision=lax.Precision.HIGHEST,
        )
        * score_scale
    )
    combined = within + carried
    root_mean = jnp.sqrt(jnp.mean(combined * combined, axis=-1, keepdims=True) + 1e-06)
    normed = combined / root_mean * lin_gain.reshape(heads_here, HEAD)
    return normed.reshape(length, heads_here * HEAD).astype(jnp.bfloat16)


def experts_layer(moe_input, routes, route_weight, gate_weight, up_weight, down_weight):
    row_count = moe_input.shape[0]
    pair_count = row_count * TOP
    flat_ids = routes.reshape(pair_count)
    same_expert = flat_ids[:, None] == flat_ids[None, :]
    pair_order = jnp.arange(pair_count, dtype=jnp.int32)
    earlier_pair = pair_order[None, :] < pair_order[:, None]
    slot_rank = jnp.sum(jnp.logical_and(same_expert, earlier_pair), axis=1)
    slot_index = slot_rank * EXPERTS + flat_ids
    onehot = (slot_index[None, :] == jnp.arange(CAP * EXPERTS, dtype=jnp.int32)[:, None]).astype(
        jnp.bfloat16
    )
    pair_rows = jnp.repeat(moe_input, TOP, axis=0)
    outgoing = (
        jnp.dot(onehot, pair_rows, preferred_element_type=jnp.float32)
        .astype(jnp.bfloat16)
        .reshape(CAP, EXPERTS, D)
    )
    arrived = lax.all_to_all(outgoing, "exp", split_axis=1, concat_axis=0, tiled=True)
    shard_piece = lax.all_gather(arrived, "ctx", axis=0, tiled=True)
    gate_part = jnp.einsum(
        "red,edf->ref", shard_piece, gate_weight, preferred_element_type=jnp.float32
    )
    up_part = jnp.einsum("red,edf->ref", shard_piece, up_weight, preferred_element_type=jnp.float32)
    hidden = (jax.nn.silu(gate_part) * up_part).astype(jnp.bfloat16)
    expert_out = lax.psum_scatter(
        jnp.einsum("ref,efd->red", hidden, down_weight, preferred_element_type=jnp.float32),
        "ctx",
        scatter_dimension=0,
        tiled=True,
    ).astype(jnp.bfloat16)
    returned = lax.all_to_all(expert_out, "exp", split_axis=0, concat_axis=1, tiled=True).reshape(
        CAP * EXPERTS, D
    )
    pair_out = jnp.dot(onehot.T, returned, preferred_element_type=jnp.float32).reshape(
        row_count, TOP, D
    )
    mixed = jnp.sum(pair_out * route_weight[:, :, None], axis=1)
    return mixed.astype(jnp.bfloat16)


def softmax_layer(soft_query, soft_kv):
    length = soft_query.shape[0]
    kv_here = soft_kv.shape[1]
    group = HEAD_TOTAL // KV_HEADS
    score_scale = 1.0 / math.sqrt(HEAD)
    queries = soft_query.reshape(length, kv_here, group, HEAD)
    query_pos = lax.axis_index("ctx") * length + jnp.arange(length, dtype=jnp.int32)
    shard_piece = lax.all_gather(soft_kv, "ctx", axis=0, tiled=True)
    maxima = jnp.full((kv_here, group, length), -jnp.inf, jnp.float32)
    totals = jnp.zeros((kv_here, group, length), jnp.float32)
    running = jnp.zeros((kv_here, group, length, HEAD), jnp.float32)
    key_rows = shard_piece[:, :, 0, :]
    value_rows = shard_piece[:, :, 1, :]
    key_pos = jnp.arange(shard_piece.shape[0], dtype=jnp.int32)
    scores = (
        jnp.einsum("tghd,jgd->ghtj", queries, key_rows, preferred_element_type=jnp.float32)
        * score_scale
    )
    allowed = key_pos[None, :] <= query_pos[:, None]
    scores = jnp.where(allowed[None, None], scores, -jnp.inf)
    new_max = jnp.max(scores, axis=-1)
    safe_max = jnp.where(jnp.isfinite(new_max), new_max, 0.0)
    shrink = jnp.exp(maxima - safe_max)
    weights = jnp.exp(scores - safe_max[..., None])
    totals = totals * shrink + jnp.sum(weights, axis=-1)
    update = jnp.einsum(
        "ghtj,jgd->ghtd",
        weights.astype(jnp.bfloat16),
        value_rows,
        preferred_element_type=jnp.float32,
    )
    running = running * shrink[..., None] + update
    output = running / totals[..., None]
    return output.transpose(2, 0, 1, 3).reshape(length, kv_here * group * HEAD).astype(jnp.bfloat16)


def on_device(
    lin_query,
    lin_key,
    lin_value,
    log_decay,
    lin_gain,
    moe_input,
    routes,
    route_weight,
    gate_weight,
    up_weight,
    down_weight,
    soft_query,
    soft_kv,
):
    lin_out = lightning(lin_query, lin_key, lin_value, log_decay, lin_gain)
    soft_out = softmax_layer(soft_query, soft_kv)
    moe_out = experts_layer(moe_input, routes, route_weight, gate_weight, up_weight, down_weight)
    return (lin_out, moe_out, soft_out)


def solution(mesh):
    placed = (
        P("ctx", "exp"),
        P("ctx", "exp"),
        P("ctx", "exp"),
        P("ctx", "exp"),
        P("exp"),
        P(("ctx", "exp"), None),
        P(("ctx", "exp"), None),
        P(("ctx", "exp"), None),
        P("exp", None, "ctx"),
        P("exp", None, "ctx"),
        P("exp", "ctx", None),
        P("ctx", "exp"),
        P("ctx", "exp", None, None),
    )
    return jax.shard_map(
        on_device,
        mesh=mesh,
        in_specs=placed,
        out_specs=(P("ctx", "exp"), P(("ctx", "exp"), None), P("ctx", "exp")),
        check_vma=False,
    )
```

profile of v0, /device:TPU:1, one launch (start us, length us, event | category | flops | bytes accessed | tf_op | source)
XLA Modules:
  0.0 780.1 jit_solution(14892325670164838628)
XLA Ops:
  13.0 18.5 %all_to_all.33 = bf16[2,8,6144]{2,0,1:T(2,128)(2,1)} all-to-all(bf16[2,8,6144]{2,0,1:T(2,128)(2,1)S(1)} %copy.120), channel_id=1, replica_groups=mesh['ctx'=32,'exp'=8] {'exp'}, dimensions={1} | all-to-all | bytes 393216 | tf_op jit(solution)/shard_map/all_to_all | solution.py:98
  43.3 2.2 fusion.56
  45.6 132.8 %all-gather.6.cloned.1.call-done = bf16[512,1,6144]{2,0,1:T(8,128)(2,1)} async-done(((bf16[16,1,6144]{2,0,1:T(8,128)(2,1)}), bf16[512,1,6144]{2,0,1:T(8,128)(2,1)}) %all-gather.6.cloned.1.call-update) | async-done | bytes 6291472 | tf_op jit(solution)/shard_map/all_gather | solution.py:99
  178.4 6.0 fusion.16
  187.1 6.4 convolution_bitcast_fusion
  194.6 68.3 %all-gather.1 = f32[32,1,8]{2,1,0:T(1,128)} all-gather(f32[1,1,8]{2,1,0:T(1,128)S(1)} %copy-done.7), channel_id=1, replica_groups=mesh['ctx'=32,'exp'=8] {'ctx'}, dimensions={0}, use_global_device_ids=true | all-gather | bytes 1056 | tf_op jit(solution)/shard_map/all_gather | solution.py:19
  264.4 69.8 %all-gather.8.cloned.1.call-done = bf16[4096,1,2,128]{3,0,2,1:T(8,128)(2,1)} async-done(((bf16[128,1,2,128]{3,0,2,1:T(8,128)(2,1)}), bf16[4096,1,2,128]{3,0,2,1:T(8,128)(2,1)}) %all-gather.8.cloned.1.call-update) | async-done | bytes 2097168 | tf_op jit(solution)/shard_map/all_gather | solution.py:128
  334.2 8.2 %fusion.3 = (f32[8,128]{1,0:T(8,128)S(1)}, f32[4096,128,8]{1,0,2:T(8,128)}) fusion(pred[128,4096]{0,1:T(8,128)(4,1)S(1)} %iota_compare_fusion, bf16[4096,1,2,128]{3,0,2,1:T(8,128)(2,1)} %all-gather.8.cloned.1.call-done, bf16[128,1024]{1,0:T(8,128)(2,1)S(1)} %copy-done.11), kind=kOutput, calls=%fused_computation.7 | convolution fusion | flops 1086323712 | bytes 18616320 | tf_op jit(solution)/shard_map/tghd,jgd->ghtj/dot_general | solution.py:136
  342.4 9.3 %fusion.1 = f32[8,128]{1,0:T(8,128)S(1)} fusion(f32[4096,128,8]{1,0,2:T(8,128)} %get-tuple-element.152, f32[8,128]{1,0:T(8,128)S(1)} %is-finite_select_fusion, pred[128,4096]{0,1:T(8,128)(4,1)S(1)} %iota_compare_fusion), kind=kLoop, calls=%fused_computation.5 | loop fusion | flops 16776192 | bytes 17309696 | tf_op jit(solution)/shard_map/reduce_sum | solution.py:145
  351.8 8.6 %fusion.53 = bf16[8,128,128]{1,2,0:T(8,128)(2,1)} fusion(bf16[4096,1,2,128]{3,0,2,1:T(8,128)(2,1)S(1)} %copy-done.10, f32[4096,128,8]{1,0,2:T(8,128)} %get-tuple-element.152, f32[8,128]{1,0:T(8,128)S(1)} %is-finite_select_fusion, pred[128,4096]{0,1:T(8,128)(4,1)S(1)} %iota_compare_fusion, f32[8,128]{1,0:T(8,128)S(1)} %get-tuple-element.146, ...), kind=kOutput, calls=%fused_computation.41 | convolution fusion | flops 1090912256 | bytes 18624512 | tf_op jit(solution)/shard_map/ghtj,jgd->ghtd/dot_general | solution.py:146
  362.3 183.9 %all-gather.10.cloned.1.call-done = f32[256,128,128]{2,1,0:T(8,128)} async-done(((f32[8,128,128]{2,1,0:T(8,128)}), f32[256,128,128]{2,1,0:T(8,128)}) %all-gather.10.cloned.1.call-update) | async-done | bytes 16777232 | tf_op jit(solution)/shard_map/all_gather | solution.py:19
  546.2 87.4 %while.14 = (s32[]{:T(128)}, f32[8,128,128]{2,1,0:T(8,128)}, s32[]{:T(128)}, f32[32,8]{1,0:T(8,128)}, f32[32,8,128,128]{3,2,1,0:T(8,128)}, /*index=5*/s32[]{:T(128)}, s32[]{:T(128)}) while((s32[]{:T(128)}, f32[8,128,128]{2,1,0:T(8,128)}, s32[]{:T(128)}, f32[32,8]{1,0:T(8,128)}, f32[32,8,128,128]{3,2,1,0:T(8,128)}, ...), condition=%wide.region_2.3_spmd.clone, body=%wide.region_1.2_spmd.clone.sunk | while | flops 524292 | bytes 1573065 | solution.py:28
  549.5 2.1 fusion.93
  552.4 2.1 fusion.93
  555.2 2.1 fusion.93
  558.0 2.1 fusion.93
  560.8 2.1 fusion.93
  563.6 2.1 fusion.93
  566.5 2.1 fusion.93
  569.3 2.1 fusion.93
  572.1 2.1 fusion.93
  575.0 2.1 fusion.93
  577.8 2.1 fusion.93
  580.6 2.1 fusion.93
  583.4 2.1 fusion.93
  586.3 2.1 fusion.93
  589.1 2.1 fusion.93
  591.9 2.1 fusion.93
  594.8 2.1 fusion.93
  597.6 2.1 fusion.93
  600.4 2.1 fusion.93
  603.2 2.1 fusion.93
  608.9 2.1 fusion.93
  611.7 2.1 fusion.93
  614.5 2.1 fusion.93
  617.3 2.1 fusion.93
  620.1 2.1 fusion.93
  623.0 2.1 fusion.93
  625.8 2.1 fusion.93
  628.6 2.1 fusion.93
  631.4 2.1 fusion.93
  635.3 2.6 multiply_reduce_fusion
  637.9 84.6 %reduce-scatter.2.cloned.1.call-done = f32[16,1,6144]{2,0,1:T(8,128)} async-done(((f32[512,1,6144]{2,0,1:T(8,128)}), f32[16,1,6144]{2,0,1:T(8,128)}) %reduce-scatter.2.cloned.1.call-update) | async-done | bytes 393232 | tf_op jit(solution)/shard_map/reduce_scatter | solution.py:105
  724.7 2.3 reduce.3
  728.8 27.5 %all-to-all-start.1 = ((bf16[8,2,6144]{2,1,0:T(2,128)(2,1)}), bf16[8,2,6144]{2,1,0:T(2,128)(2,1)}, u32[]{:S(2)}, u32[]{:S(2)}) async-start(bf16[8,2,6144]{2,1,0:T(2,128)(2,1)} %reshape.218), calls=%async_computation.2 | async-start | bytes 393216 | tf_op jit(solution)/shard_map/all_to_all | solution.py:111
  760.0 5.0 all-to-all-done.1
  764.9 2.2 reshape.219
  767.2 2.8 reduce.2
  (104 shorter events, 63.1 us)
Async XLA Ops:
  7.2 179.9 %copy-start = (bf16[1,288,6144]{2,1,0:T(8,128)(2,1)S(1)}, bf16[1,288,6144]{2,1,0:T(8,128)(2,1)}, u32[]{:S(2)}) copy-start(bf16[1,288,6144]{2,1,0:T(8,128)(2,1)} %param.25) | copy-start | bytes 10616836
  7.2 171.2 %all-gather.6.cloned.1.call-start = ((), (), s32[]{:S(2)}) async-start(), calls=%async_computation.3 | async-start | bytes 6488064 | tf_op jit(solution)/shard_map/all_gather | solution.py:99
  33.3 301.0 %all-gather.8.cloned.1.call-start = ((), (), s32[]{:S(2)}) async-start(), calls=%async_computation.5 | async-start | bytes 2162688 | tf_op jit(solution)/shard_map/all_gather | solution.py:128
  34.8 511.4 %all-gather.10.cloned.1.call-start = ((), (), s32[]{:S(2)}) async-start(), calls=%async_computation.6 | async-start | bytes 17301504 | tf_op jit(solution)/shard_map/all_gather | solution.py:19
  45.6 676.9 %reduce-scatter.2.cloned.1.call-start = ((), (), s32[]{:S(2)}) async-start(), calls=%async_computation.4 | async-start | bytes 12976128 | tf_op jit(solution)/shard_map/reduce_scatter | solution.py:105
  178.4 6.0 copy-start.8
  178.4 6.6 copy-start.9
  193.5 0.8 copy-start.5
  193.5 0.9 copy-start.3
  193.5 1.1 copy-start.7
  193.5 69.5 %copy-start.2 = (bf16[128,1024]{0,1:T(8,128)(2,1)S(1)}, bf16[128,1024]{0,1:T(8,128)(2,1)}, u32[]{:S(2)}) copy-start(bf16[128,1024]{0,1:T(8,128)(2,1)} %copy.134) | copy-start | bytes 786436
  193.5 69.5 %copy-start.4 = (bf16[128,1024]{1,0:T(8,128)(2,1)S(1)}, bf16[128,1024]{1,0:T(8,128)(2,1)}, u32[]{:S(2)}) copy-start(bf16[128,1024]{1,0:T(8,128)(2,1)} %param.15) | copy-start | bytes 786436
  193.5 140.7 %copy-start.11 = (bf16[128,1024]{1,0:T(8,128)(2,1)S(1)}, bf16[128,1024]{1,0:T(8,128)(2,1)}, u32[]{:S(2)}) copy-start(bf16[128,1024]{1,0:T(8,128)(2,1)} %param.26) | copy-start | bytes 786436
  342.4 9.3 %copy-start.10 = (bf16[4096,1,2,128]{3,0,2,1:T(8,128)(2,1)S(1)}, bf16[4096,1,2,128]{3,0,2,1:T(8,128)(2,1)}, u32[]{:S(2)}) copy-start(bf16[4096,1,2,128]{3,0,2,1:T(8,128)(2,1)} %all-gather.8.cloned.1.call-done) | copy-start | bytes 6291460
  360.3 395.9 %copy-start.6 = (f32[1024]{0:T(1024)S(1)}, f32[1024]{0:T(1024)}, u32[]{:S(2)}) copy-start(f32[1024]{0:T(1024)} %param.19) | copy-start | bytes 12292
  360.3 413.2 %copy-start.1 = (bf16[1,288,6144]{2,1,0:T(8,128)(2,1)S(1)}, bf16[1,288,6144]{2,1,0:T(8,128)(2,1)}, u32[]{:S(2)}) copy-start(bf16[1,288,6144]{2,1,0:T(8,128)(2,1)} %param.25) | copy-start | bytes 10616836
  728.8 36.2 %all-to-all-start.1 = ((bf16[8,2,6144]{2,1,0:T(2,128)(2,1)}), bf16[8,2,6144]{2,1,0:T(2,128)(2,1)}, u32[]{:S(2)}, u32[]{:S(2)}) async-start(bf16[8,2,6144]{2,1,0:T(2,128)(2,1)} %reshape.218), calls=%async_computation.2 | async-start | bytes 393216 | tf_op jit(solution)/shard_map/all_to_all | solution.py:111
Sparse Core Ops, SparseCore 0:
  33.4 144.9 all-gather.5
  180.2 153.9 all-gather.7
  336.0 210.1 all-gather.9
  548.6 173.8 reduce-scatter.1
where the time goes:
time: 783 us; the launch traced here: 780 us
  waiting for transfers between devices  476 us (61%)
  other arithmetic  87.9 us (11%)
  blocking collectives  86.9 us (11%)
  local copies, waits for them, and re-layouts  45.9 us (6%)
  matrix products  41.8 us (5%)
  starting transfers between devices  27.6 us (4%)
  between operations  13.9 us (2%)
    all_gather x1, waiting for transfers between devices, prefix(): pieces = jax.tree.map(lambda part: lax.all_gather(part, axis), value)  184 us
    all_gather x1, waiting for transfers between devices, experts_layer(): shard_piece = lax.all_gather(arrived, 'ctx', axis=0, tiled=True)  133 us
    reduce_scatter x1, waiting for transfers between devices, experts_layer(): lax.psum_scatter(jnp.einsum('ref,efd->red', hidden, down_weight, preferre...  84.6 us
    all_gather x1, waiting for transfers between devices, softmax_layer(): shard_piece = lax.all_gather(soft_kv, 'ctx', axis=0, tiled=True)  69.8 us
    all_gather x1, blocking collectives, prefix(): pieces = jax.tree.map(lambda part: lax.all_gather(part, axis), value)  68.3 us
    select_n x31, other arithmetic, hop(): jnp.where(position < mine, new, old)  66.2 us
    all_to_all x1, starting transfers between devices, experts_layer(): lax.all_to_all(expert_out, 'exp', split_axis=0, concat_axis=1, tiled=True)  27.5 us
    exp x31, local copies, waits for them, and re-layouts, combine(): jnp.exp(latter[0])[:, None, None] * earlier[1] + latter[1]  21.2 us
  transfers between devices with their start and end apart: 5, of which 5 were waited for; matrix products, arithmetic and copies ran while one was open for 19% of the time, Pallas kernels for 0%

commit v1 on v0

v1 whole, which is shorter than its diff:
```python
import math

import jax
import jax.numpy as jnp
from jax import lax
from jax.experimental import pallas as pl
from jax.experimental.pallas import tpu as pltpu
from jax.sharding import PartitionSpec as P

D = 6144
HEAD = 128
EXPERTS = 8
TOP = 2
CAP = 2
CTX = 32
SEQ = 128
HEADS = 8
FF = 288
ROWS = 16
SCALE = 1.0 / math.sqrt(HEAD)
F32, BF16 = jnp.float32, jnp.bfloat16
MESH = pl.DeviceIdType.MESH
DFS = (2, 1, -1, 0)


def dot(a, b, dims=((1,), (0,))):
    return lax.dot_general(a, b, (dims, ((), ())), preferred_element_type=F32)


def dot_split(a, b, dims=((1,), (0,))):
    high = a.astype(BF16)
    low = (a - high.astype(F32)).astype(BF16)
    return dot(high, b, dims) + dot(low, b, dims)


def kernel(
    slabs, kv_own, gate_hbm, up_hbm, down_hbm, lin_q, lin_k, lin_v, decay, decay_t, gain, soft_q,
    ret, lin_out, soft_out,
    kv, tok, part, s1r, s2r, f1r, f2r, zr, got, back, wide, gate, up, down, hidden,
    bias, cum, cum_t, state_out, state_in, prior_out, prior,
    w_sem, kv_send, kv_recv, tok_send, tok_recv, rs_send, s1_sem, s2_sem, f1_sem, f2_sem, z_sem,
    go_send, go_recv, back_send, back_recv, st_send, st_recv, pr_send, pr_recv,
):
    c, e = lax.axis_index("ctx"), lax.axis_index("exp")
    y, z, x, core = c // 8, (c // 4) % 2, c % 4, e % 2
    f, s = x + core * (y - x), y + core * (x - y)

    def rel(step):
        ds, df, dz = step
        return (s + ds + 4) % 4, (f + df + 4) % 4, (z + dz) % 2

    def ctx_of(step):
        ss, ff, zz = rel(step)
        return (ss + core * (ff - ss)) * 8 + zz * 4 + ff + core * (ss - ff)

    def index_of(step):
        ss, ff, zz = rel(step)
        return ss * 8 + ff * 2 + zz

    def rows_of(step, rows):
        return pl.ds(pl.multiple_of(index_of(step) * rows, rows), rows)

    barrier = pltpu.get_barrier_semaphore()

    @pl.loop(1, CTX)
    def _(k):
        pl.semaphore_signal(barrier, inc=1, device_id=((c + k) % CTX, e), device_id_type=MESH)

    @pl.loop(1, EXPERTS)
    def _(k):
        pl.semaphore_signal(barrier, inc=1, device_id=(c, (e + k) % EXPERTS), device_id_type=MESH)

    pl.semaphore_wait(barrier, CTX - 1 + EXPERTS - 1)

    weights = [
        pltpu.make_async_copy(src, dst, w_sem.at[i])
        for i, (src, dst) in enumerate(((gate_hbm, gate), (up_hbm, up), (down_hbm, down)))
    ]
    for copy in weights:
        copy.start()

    unfinished = []

    def push(src, dst, send_sem, recv_sem, to):
        copy = pltpu.make_async_remote_copy(
            src_ref=src, dst_ref=dst, send_sem=send_sem, recv_sem=recv_sem, device_id=to, device_id_type=MESH
        )
        copy.start()
        unfinished.append(copy)

    def landed(ref, recv_sem, spare_sem):
        pltpu.make_async_remote_copy(
            src_ref=ref, dst_ref=ref, send_sem=spare_sem, recv_sem=recv_sem,
            device_id=(ctx_of((0, 0, 1)), e), device_id_type=MESH,
        ).wait_recv()

    def gather(buf, rows, send_sems, recv_sems):
        used = [0]

        def send(step, to):
            where = rows_of(step, rows)
            push(buf.at[where], buf.at[where], send_sems.at[used[0]], recv_sems.at[index_of(step)], (ctx_of(to), e))
            used[0] += 1

        def sideways(step):
            send(step, (1, 0, 0))
            send(step, (-1, 0, 0))

        def own():
            send((0, 0, 0), (0, 0, 1))
            send((0, 0, 0), (0, 1, 0))
            send((0, 0, 0), (0, -1, 0))
            sideways((0, 0, 0))

        def arrive(*steps):
            for step in steps:
                ds, df, dz = step
                landed(buf.at[rows_of(step, rows)], recv_sems.at[index_of(step)], send_sems.at[0])
                if ds == 0:
                    if df == 0:
                        send(step, (0, 1, 0))
                        send(step, (0, -1, 0))
                    elif df == -1 and dz == 0:
                        send(step, (0, 1, 0))
                    elif df == 1 and dz == 1:
                        send(step, (0, -1, 0))
                    sideways(step)
                elif ds == -1 and dz == 0:
                    send(step, (1, 0, 0))
                elif ds == 1 and dz == 1:
                    send(step, (-1, 0, 0))

        return own, arrive

    kv_first, kv_arrive = gather(kv, SEQ, kv_send, kv_recv)
    tok_first, tok_arrive = gather(tok, ROWS, tok_send, tok_recv)

    @pl.loop(1, EXPERTS)
    def _(k):
        to = (e + k) % EXPERTS
        pltpu.make_async_remote_copy(
            src_ref=slabs.at[to], dst_ref=got.at[e], send_sem=go_send.at[to], recv_sem=go_recv.at[e],
            device_id=(c, to), device_id_type=MESH,
        ).start()

    kv[rows_of((0, 0, 0), SEQ), :] = kv_own[...]
    kv_first()

    row = lax.broadcasted_iota(jnp.int32, (SEQ, SEQ), 0)
    col = lax.broadcasted_iota(jnp.int32, (SEQ, SEQ), 1)
    lower = (col <= row).astype(BF16)

    def three(a):
        high = a.astype(BF16)
        mid = (a - high.astype(F32)).astype(BF16)
        low = (a - high.astype(F32) - mid.astype(F32)).astype(BF16)
        return high, mid, low

    cum[...] = sum(dot(lower, term) for term in three(decay[...]))
    cum_t[...] = sum(dot(term, lower, ((1,), (1,))) for term in three(decay_t[...]))
    last = cum[SEQ - 1 : SEQ, :]
    line = lax.broadcasted_iota(jnp.int32, (16, HEAD), 0)
    for h in range(HEADS):
        tail = jnp.exp(last[:, h : h + 1] - cum[:, h : h + 1])
        head = pl.ds(h * HEAD, HEAD)
        scaled = lin_k[:, head].astype(F32) * tail
        state = dot_split(scaled.T, lin_v[:, head])
        high, mid, low = (jnp.broadcast_to(t.astype(F32), (16, HEAD)) for t in three(last[:, h : h + 1]))
        logs = jnp.where(line == 0, high, jnp.where(line == 1, mid, jnp.where(line == 2, low, 0.0))).astype(BF16)
        for i in range(4):
            state_out[4 * h + i, 0:32, :] = state[32 * i : 32 * i + 32].astype(BF16)
            state_out[4 * h + i, 32:48, :] = logs

    @pl.loop(1, CTX)
    def _(k):
        to = (c + k) % CTX
        pltpu.make_async_remote_copy(
            src_ref=state_out.at[to], dst_ref=state_in.at[c], send_sem=st_send.at[to], recv_sem=st_recv.at[c],
            device_id=(to, e), device_id_type=MESH,
        ).start()

    state_in[c] = state_out[c]

    kv_arrive((0, 0, 1), (0, 1, 0), (0, -1, 0), (1, 0, 0), (-1, 0, 0))

    got[e] = slabs[e]

    @pl.loop(1, EXPERTS)
    def _(k):
        at = (e + k) % EXPERTS
        pltpu.make_async_remote_copy(
            src_ref=slabs.at[at], dst_ref=got.at[at], send_sem=go_send.at[at], recv_sem=go_recv.at[at],
            device_id=(c, at), device_id_type=MESH,
        ).wait()

    for i in range(EXPERTS):
        wide[2 * i : 2 * i + 2, :] = got[i].astype(F32)
    tok[rows_of((0, 0, 0), ROWS), :] = wide[...].astype(BF16)
    tok_first()

    kv_arrive((0, 1, 1), (0, -1, 1), (1, 0, 1), (-1, 0, 1), (0, 2, 0), (0, 2, 1))
    kv_arrive(*((ds, df, 0) for df in (1, -1) for ds in (1, -1)))
    tok_arrive((0, 0, 1), (0, 1, 0), (0, -1, 0), (1, 0, 0), (-1, 0, 0))
    kv_arrive(*((ds, df, 1) for df in (1, -1) for ds in (1, -1)))
    kv_arrive(*((ds, 2, dz) for dz in (0, 1) for ds in (1, -1)))
    kv_arrive(*((2, df, dz) for df in (0, 1, -1, 2) for dz in (0, 1)))
    tok_arrive((0, 1, 1), (0, -1, 1))

    @pl.loop(1, CTX)
    def _(k):
        at = (c + k) % CTX
        pltpu.make_async_remote_copy(
            src_ref=state_out.at[at], dst_ref=state_in.at[at], send_sem=st_send.at[at], recv_sem=st_recv.at[at],
            device_id=(at, e), device_id_type=MESH,
        ).wait()

    def hop(i, run):
        prior_out[i] = run.astype(BF16)
        logs = jnp.sum(state_in[i, 32:48, :].astype(F32), axis=0, keepdims=True)
        return jnp.exp(logs) * run + state_in[i, 0:32, :].astype(F32)

    lax.fori_loop(0, CTX, hop, jnp.zeros((32, HEAD), F32))

    @pl.loop(1, CTX)
    def _(k):
        to = (c + k) % CTX
        pltpu.make_async_remote_copy(
            src_ref=prior_out.at[to], dst_ref=prior.at[c], send_sem=pr_send.at[to], recv_sem=pr_recv.at[c],
            device_id=(to, e), device_id_type=MESH,
        ).start()

    prior[c] = prior_out[c]

    wide_col = lax.broadcasted_iota(jnp.int32, (8, CTX * SEQ), 1)
    blk = jnp.right_shift(wide_col, 7)
    b_s, b_f, b_z = jnp.right_shift(blk, 3), jnp.bitwise_and(jnp.right_shift(blk, 1), 3), jnp.bitwise_and(blk, 1)
    b_ctx = (b_s + core * (b_f - b_s)) * 8 + b_z * 4 + b_f + core * (b_s - b_f)
    place = b_ctx * SEQ + jnp.bitwise_and(wide_col, SEQ - 1)
    line8 = lax.broadcasted_iota(jnp.int32, (8, CTX * SEQ), 0)

    @pl.loop(0, SEQ // 8)
    def _(i):
        bias[pl.ds(pl.multiple_of(i * 8, 8), 8), :] = jnp.where(place <= c * SEQ + i * 8 + line8, 0.0, -1e30)

    def attend(first, count):
        @pl.loop(first, first + count)
        def _(h):
            head = pl.ds(pl.multiple_of(h * HEAD, HEAD), HEAD)
            scores = dot(soft_q[:, head], kv[:, 0:HEAD], ((1,), (1,))) * SCALE + bias[...]
            top = jnp.max(scores, axis=1, keepdims=True)
            probs = jnp.exp(scores - top)
            total = jnp.sum(probs, axis=1, keepdims=True)
            mixed = dot(probs.astype(BF16), kv[:, HEAD : 2 * HEAD])
            soft_out[:, head] = (mixed / total).astype(BF16)

    def finish_lightning(heads):
        for h in heads:
            head = pl.ds(h * HEAD, HEAD)
            here = cum[:, h : h + 1]
            spread = here - cum_t[h : h + 1, :]
            decays = jnp.where(col <= row, jnp.exp(jnp.where(col <= row, spread, 0.0)), 0.0)
            scores = dot(lin_q[:, head], lin_k[:, head], ((1,), (1,))) * SCALE
            within = dot_split(scores * decays, lin_v[:, head])
            before = prior[4 * h : 4 * h + 4].reshape(HEAD, HEAD)
            combined = within + jnp.exp(here) * dot(lin_q[:, head], before) * SCALE
            root = jnp.sqrt(jnp.mean(combined * combined, axis=1, keepdims=True) + 1e-06)
            lin_out[:, head] = (combined / root * gain[:, head]).astype(BF16)

    chunk = 1024

    def group(ds):
        return pl.ds(pl.multiple_of((s + ds + 4) % 4 * 8 * ROWS, 8 * ROWS), 8 * ROWS)

    def enter(ds):
        def add(k, sums):
            at = pl.ds(pl.multiple_of(k * chunk, chunk), chunk)
            tokens = tok[group(ds), at]
            return sums[0] + dot(tokens, gate[at, :]), sums[1] + dot(tokens, up[at, :])

        zero = jnp.zeros((8 * ROWS, FF), F32)
        a, b = lax.fori_loop(0, D // chunk, add, (zero, zero))
        hidden[group(ds), :] = (a / (1.0 + jnp.exp(-a)) * b).astype(BF16)

    def leave(ds):
        @pl.loop(0, D // chunk)
        def _(k):
            at = pl.ds(pl.multiple_of(k * chunk, chunk), chunk)
            part[group(ds), at] = dot(hidden[group(ds), :], down[:, at]).astype(BF16)

    attend(0, 1)
    tok_arrive((1, 0, 1), (-1, 0, 1), (0, 2, 0), (0, 2, 1))
    attend(1, 1)
    tok_arrive(*((ds, df, 0) for df in (1, -1) for ds in (1, -1)))
    attend(2, 1)
    attend(3, 1)
    tok_arrive(*((ds, df, 1) for df in (1, -1) for ds in (1, -1)))
    attend(4, 2)
    for copy in weights:
        copy.wait()
    enter(0)
    tok_arrive(*((ds, 2, dz) for dz in (0, 1) for ds in (1, -1)))
    attend(6, 2)
    enter(1)
    enter(-1)
    tok_arrive(*((2, df, dz) for df in (0, 1, -1, 2) for dz in (0, 1)))
    enter(2)

    rs_used = [0]

    def send_part(step, dst, sem, to):
        push(part.at[rows_of(step, ROWS)], dst, rs_send.at[rs_used[0]], sem, (ctx_of(to), e))
        rs_used[0] += 1

    def block(ref, i):
        return ref.at[pl.ds(i * ROWS, ROWS)]

    def add_in(step, *blocks):
        where = rows_of(step, ROWS)
        total = part[where, :].astype(F32)
        for b in blocks:
            total = total + b[...].astype(F32)
        part[where, :] = total.astype(BF16)

    leave(2)
    for i, df in enumerate(DFS):
        send_part((2, df, 0), block(s1r, 2 * i), s1_sem.at[2 * i], (-1, 0, 0))
        send_part((2, df, 1), block(s1r, 2 * i + 1), s1_sem.at[2 * i + 1], (1, 0, 0))
    leave(-1)
    for i, df in enumerate(DFS):
        send_part((-1, df, 1), block(s2r, 4 * i + 1), s2_sem.at[4 * i + 1], (-1, 0, 0))
    leave(1)
    for i, df in enumerate(DFS):
        send_part((1, df, 0), block(s2r, 4 * i + 2), s2_sem.at[4 * i + 2], (1, 0, 0))
    leave(0)

    @pl.loop(1, CTX)
    def _(k):
        at = (c + k) % CTX
        pltpu.make_async_remote_copy(
            src_ref=prior_out.at[at], dst_ref=prior.at[at], send_sem=pr_send.at[at], recv_sem=pr_recv.at[at],
            device_id=(at, e), device_id_type=MESH,
        ).wait()

    for i, df in enumerate(DFS):
        for k, step, to in ((0, (-1, df, 0), (-1, 0, 0)), (1, (1, df, 1), (1, 0, 0))):
            landed(block(s1r, 2 * i + k), s1_sem.at[2 * i + k], rs_send.at[0])
            add_in(step, block(s1r, 2 * i + k))
            slot = 4 * i + (0 if k == 0 else 3)
            send_part(step, block(s2r, slot), s2_sem.at[slot], to)
        finish_lightning((2 * i, 2 * i + 1))

    for i, df in enumerate(DFS):
        for slot in (1, 2, 0, 3):
            landed(block(s2r, 4 * i + slot), s2_sem.at[4 * i + slot], rs_send.at[0])
        add_in((0, df, 0), block(s2r, 4 * i), block(s2r, 4 * i + 2))
        add_in((0, df, 1), block(s2r, 4 * i + 1), block(s2r, 4 * i + 3))
        if df == 2:
            send_part((0, 2, 0), block(f1r, 0), f1_sem.at[0], (0, -1, 0))
            send_part((0, 2, 1), block(f1r, 1), f1_sem.at[1], (0, 1, 0))
        elif df == 1:
            send_part((0, 1, 0), block(f2r, 2), f2_sem.at[2], (0, 1, 0))
        elif df == -1:
            send_part((0, -1, 1), block(f2r, 1), f2_sem.at[1], (0, -1, 0))
            for k, step, to in ((0, (0, -1, 0), (0, -1, 0)), (1, (0, 1, 1), (0, 1, 0))):
                landed(block(f1r, k), f1_sem.at[k], rs_send.at[0])
                add_in(step, block(f1r, k))
                slot = 0 if k == 0 else 3
                send_part(step, block(f2r, slot), f2_sem.at[slot], to)

    landed(block(f2r, 1), f2_sem.at[1], rs_send.at[0])
    landed(block(f2r, 3), f2_sem.at[3], rs_send.at[0])
    add_in((0, 0, 1), block(f2r, 1), block(f2r, 3))
    send_part((0, 0, 1), zr, z_sem.at[0], (0, 0, 1))
    landed(block(f2r, 0), f2_sem.at[0], rs_send.at[0])
    landed(block(f2r, 2), f2_sem.at[2], rs_send.at[0])
    wide[...] = (
        part[rows_of((0, 0, 0), ROWS), :].astype(F32)
        + block(f2r, 0)[...].astype(F32)
        + block(f2r, 2)[...].astype(F32)
    )
    landed(zr, z_sem.at[0], rs_send.at[0])
    wide[...] = wide[...] + zr[...].astype(F32)

    for i in range(EXPERTS):
        back[i] = wide[2 * i : 2 * i + 2, :].astype(BF16)

    @pl.loop(1, EXPERTS)
    def _(k):
        to = (e + k) % EXPERTS
        pltpu.make_async_remote_copy(
            src_ref=back.at[to], dst_ref=ret.at[e], send_sem=back_send.at[to], recv_sem=back_recv.at[e],
            device_id=(c, to), device_id_type=MESH,
        ).start()

    ret[e] = back[e]

    @pl.loop(1, EXPERTS)
    def _(k):
        at = (e + k) % EXPERTS
        pltpu.make_async_remote_copy(
            src_ref=back.at[at], dst_ref=ret.at[at], send_sem=back_send.at[at], recv_sem=back_recv.at[at],
            device_id=(c, at), device_id_type=MESH,
        ).wait()

    for copy in unfinished:
        copy.wait_send()


def on_device(
    lin_query,
    lin_key,
    lin_value,
    log_decay,
    lin_gain,
    moe_input,
    routes,
    route_weight,
    gate_weight,
    up_weight,
    down_weight,
    soft_query,
    soft_kv,
):
    rows = moe_input.shape[0]
    pairs = rows * TOP
    flat = routes.reshape(pairs)
    order = jnp.arange(pairs, dtype=jnp.int32)
    rank = jnp.sum((flat[:, None] == flat[None, :]) & (order[None, :] < order[:, None]), axis=1)
    slot = (flat * CAP + rank).reshape(rows, TOP)
    chosen = slot[None] == jnp.arange(CAP * EXPERTS, dtype=jnp.int32)[:, None, None]
    pick = jnp.any(chosen, axis=2).astype(BF16)
    slabs = jnp.dot(pick, moe_input, preferred_element_type=F32).astype(BF16).reshape(EXPERTS, CAP, D)

    vmem, any_ = pl.BlockSpec(memory_space=pltpu.VMEM), pl.BlockSpec(memory_space=pl.ANY)
    dma = pltpu.SemaphoreType.DMA
    ret, lin_out, soft_out = pl.pallas_call(
        kernel,
        out_shape=(
            jax.ShapeDtypeStruct((EXPERTS, CAP, D), BF16),
            jax.ShapeDtypeStruct((SEQ, HEADS * HEAD), BF16),
            jax.ShapeDtypeStruct((SEQ, HEADS * HEAD), BF16),
        ),
        in_specs=[vmem, vmem, any_, any_, any_] + [vmem] * 7,
        out_specs=(vmem, vmem, vmem),
        scratch_shapes=[
            pltpu.VMEM((CTX * SEQ, 2 * HEAD), BF16),
            pltpu.VMEM((CTX * ROWS, D), BF16),
            pltpu.VMEM((CTX * ROWS, D), BF16),
            pltpu.VMEM((8 * ROWS, D), BF16),
            pltpu.VMEM((16 * ROWS, D), BF16),
            pltpu.VMEM((2 * ROWS, D), BF16),
            pltpu.VMEM((4 * ROWS, D), BF16),
            pltpu.VMEM((ROWS, D), BF16),
            pltpu.VMEM((EXPERTS, CAP, D), BF16),
            pltpu.VMEM((EXPERTS, CAP, D), BF16),
            pltpu.VMEM((ROWS, D), F32),
            pltpu.VMEM((D, FF), BF16),
            pltpu.VMEM((D, FF), BF16),
            pltpu.VMEM((FF, D), BF16),
            pltpu.VMEM((CTX * ROWS, FF), BF16),
            pltpu.VMEM((SEQ, CTX * SEQ), F32),
            pltpu.VMEM((SEQ, HEADS), F32),
            pltpu.VMEM((HEADS, SEQ), F32),
            pltpu.VMEM((CTX, 48, HEAD), BF16),
            pltpu.VMEM((CTX, 48, HEAD), BF16),
            pltpu.VMEM((CTX, 32, HEAD), BF16),
            pltpu.VMEM((CTX, 32, HEAD), BF16),
            dma((3,)),
            dma((31,)), dma((32,)), dma((31,)), dma((32,)), dma((31,)),
            dma((8,)), dma((16,)), dma((2,)), dma((4,)), dma((1,)),
            dma((EXPERTS,)), dma((EXPERTS,)), dma((EXPERTS,)), dma((EXPERTS,)),
            dma((CTX,)), dma((CTX,)), dma((CTX,)), dma((CTX,)),
        ],
        compiler_params=pltpu.CompilerParams(
            collective_id=0, has_side_effects=True, vmem_limit_bytes=58 * 2**20
        ),
    )(
        slabs,
        soft_kv.reshape(SEQ, 2 * HEAD),
        gate_weight.reshape(D, FF),
        up_weight.reshape(D, FF),
        down_weight.reshape(FF, D),
        lin_query,
        lin_key,
        lin_value,
        log_decay,
        log_decay.T,
        lin_gain.reshape(1, HEADS * HEAD),
        soft_query,
    )
    mix = jnp.sum(jnp.where(chosen, route_weight[None], 0.0), axis=2)
    moe_out = lax.dot_general(
        mix, ret.reshape(CAP * EXPERTS, D).astype(F32), (((0,), (0,)), ((), ())), precision=lax.Precision.HIGHEST
    ).astype(BF16)
    return (lin_out, moe_out, soft_out)


def solution(mesh):
    placed = (
        P("ctx", "exp"),
        P("ctx", "exp"),
        P("ctx", "exp"),
        P("ctx", "exp"),
        P("exp"),
        P(("ctx", "exp"), None),
        P(("ctx", "exp"), None),
        P(("ctx", "exp"), None),
        P("exp", None, "ctx"),
        P("exp", None, "ctx"),
        P("exp", "ctx", None),
        P("ctx", "exp"),
        P("ctx", "exp", None, None),
    )
    return jax.shard_map(
        on_device,
        mesh=mesh,
        in_specs=placed,
        out_specs=(P("ctx", "exp"), P(("ctx", "exp"), None), P("ctx", "exp")),
        check_vma=False,
    )
```

time: 783 us -> 155 us (0.20)
  waiting for transfers between devices: 476 us -> 0 us
  Pallas kernels: 0 us -> 130 us
  other arithmetic: 87.9 us -> 0.38 us
  blocking collectives: 86.9 us -> 0 us
  matrix products: 41.8 us -> 1.12 us
  starting transfers between devices: 27.6 us -> 0 us
  local copies, waits for them, and re-layouts: 45.9 us -> 22.4 us
  between operations: 13.9 us -> 0.67 us
    all_gather x3 -> x0, waiting for transfers between devices: 386 us -> none  [the longest x1 184 us: prefix(): pieces = jax.tree.map(lambda part: lax.all_gather(part, axis), value)]
    pallas_call x0 -> x1, Pallas kernels: none -> 130 us  [on_device(): pl.pallas_call(kernel, out_shape=(jax.ShapeDtypeStruct((EXPERTS, CAP, D),...]
    reduce_scatter x1 -> x0, waiting for transfers between devices: 84.6 us -> none  [experts_layer(): lax.psum_scatter(jnp.einsum('ref,efd->red', hidden, down_weight, preferre...]
    all_gather x1 -> x0, blocking collectives: 68.3 us -> none  [prefix(): pieces = jax.tree.map(lambda part: lax.all_gather(part, axis), value)]
    select_n x32 -> x0, other arithmetic: 66.2 us -> none  [the longest x31 66.2 us: hop(): jnp.where(position < mine, new, old)]
    dot_general x11 -> x2, matrix products: 41.8 us -> 1.12 us  [the longest x1 0.87 us: on_device(): lax.dot_general(mix, ret.reshape(CAP * EXPERTS, D).astype(F32), (((0,), (...]
    all_to_all x1 -> x0, starting transfers between devices: 27.5 us -> none  [experts_layer(): lax.all_to_all(expert_out, 'exp', split_axis=0, concat_axis=1, tiled=True)]
    exp x33 -> x0, local copies, waits for them, and re-layouts: 22.1 us -> none  [the longest x31 21.2 us: combine(): jnp.exp(latter[0])[:, None, None] * earlier[1] + latter[1]]
  transfers between devices with their start and end apart: 5 -> 0, of which waited for: 5 -> 0; matrix products, arithmetic and copies ran while one was open for 19% -> 0% of each run, Pallas kernels for 0% -> 0%
where the time goes in v1:
time: 155 us
  Pallas kernels  130 us (84%)
  local copies, waits for them, and re-layouts  22.4 us (14%)
    pallas_call x1, Pallas kernels, on_device(): pl.pallas_call(kernel, out_shape=(jax.ShapeDtypeStruct((EXPERTS, CAP, D),...  130 us
    unnamed x10, local copies, waits for them, and re-layouts  20.4 us

profile of v1, /device:TPU:1, one launch (start us, length us, event | category | flops | bytes accessed | tf_op | source)
XLA Modules:
  0.0 154.5 jit_solution(12407882638519223712)
XLA Ops:
  0.6 0.0 copy-start
  0.6 0.8 copy.28
  1.4 0.1 eq.28
  1.5 0.2 convert_reduce_fusion
  1.7 0.1 reduce_sum.21
  1.8 0.1 fusion.1
  1.9 0.8 copy.34
  2.7 0.1 select_reduce_fusion
  2.8 1.5 copy.38
  4.2 1.4 copy.33.decay
  5.7 0.0 copy-done
  5.7 0.3 convolution_convert_fusion
  5.9 0.8 reshape.37.slabs
  6.8 6.3 %copy.31 = bf16[1,6144,288]{2,1,0:T(8,128)(2,1)} copy(bf16[1,6144,288]{1,2,0:T(8,128)(2,1)} %param.21) | data formatting | bytes 7077888 | tf_op args[8]
  13.0 6.4 %copy.32 = bf16[1,6144,288]{2,1,0:T(8,128)(2,1)} copy(bf16[1,6144,288]{1,2,0:T(8,128)(2,1)} %param.22) | data formatting | bytes 7077888 | tf_op args[9]
  19.4 129.9 %shard_map.148 = (bf16[8,2,6144]{2,1,0:T(2,128)(2,1)}, bf16[128,1024]{1,0:T(8,128)(2,1)}, bf16[128,1024]{1,0:T(8,128)(2,1)}) custom-call(bf16[8,2,6144]{2,1,0:T(2,128)(2,1)} %reshape.37.slabs, bf16[128,256]{1,0:T(8,128)(2,1)} %bitcast.17, bf16[6144,288]{1,0:T(8,128)(2,1)} %bitcast.14, bf16[6144,288]{1,0:T(8,128)(2,1)} %bitcast.15, ...), custom_call_target="tpu_custom_call" | custom-call | tf_op jit(solution)/shard_map/pallas_call | solution.py:436
  149.3 1.0 reshape.43
  150.3 0.9 convolution_convert_fusion.1
  151.2 1.7 %copy.41 = bf16[128,1024]{1,0:T(8,128)(2,1)} copy(bf16[128,1024]{1,0:T(8,128)(2,1)} %get-tuple-element.12) | data formatting | bytes 524288
  152.9 1.7 %copy.42 = bf16[128,1024]{1,0:T(8,128)(2,1)} copy(bf16[128,1024]{1,0:T(8,128)(2,1)} %get-tuple-element.14) | data formatting | bytes 524288
  (1 shorter events, 0.0 us)
Async XLA Ops:
  0.6 5.0 %copy-start = (bf16[6,6144]{1,0:T(8,128)(2,1)S(1)}, bf16[6,6144]{1,0:T(8,128)(2,1)}, u32[]{:S(2)}) copy-start(bf16[6,6144]{1,0:T(8,128)(2,1)} %param.18) | copy-start | bytes 221188

commit v2 on v1

--- a/solution.py
+++ b/solution.py
@@ -33,10 +33,33 @@
     return dot(high, b, dims) + dot(low, b, dims)
 
 
+def slots_of(routes):
+    line = lax.broadcasted_iota(jnp.int32, (ROWS, 1), 0)
+    expert, place = jnp.right_shift(line, 1), jnp.bitwise_and(line, 1)
+    met = jnp.zeros((ROWS, 1), jnp.int32)
+    found = []
+    for r in range(6):
+        named = (expert == routes[0, r]) | (expert == routes[1, r])
+        found.append((expert, named & (met == place)))
+        met = met + named.astype(jnp.int32)
+    return found
+
+
+def finish(routes, weights, ret, lin, soft, lin_out, moe_out, soft_out, wide):
+    lin_out[...] = lin[...]
+    soft_out[...] = soft[...]
+    for i in range(EXPERTS):
+        wide[2 * i : 2 * i + 2, :] = ret[i].astype(F32)
+    for r, (expert, taken) in enumerate(slots_of(routes)):
+        weight = jnp.where(expert == routes[0, r], weights[0, r], weights[1, r])
+        mixed = jnp.sum(jnp.where(taken, weight, 0.0) * wide[...], axis=0, keepdims=True)
+        moe_out[r : r + 1, :] = mixed.astype(BF16)
+
+
 def kernel(
-    slabs, kv_own, gate_hbm, up_hbm, down_hbm, lin_q, lin_k, lin_v, decay, decay_t, gain, soft_q,
+    routes, moe_in, kv_own, gate_hbm, up_hbm, down_hbm, lin_q, lin_k, lin_v, decay_t, gain, soft_q,
     ret, lin_out, soft_out,
-    kv, tok, part, s1r, s2r, f1r, f2r, zr, got, back, wide, gate, up, down, hidden,
+    kv, tok, part, s1r, s2r, f1r, f2r, zr, slabs, got, back, wide, gate, up, down, hidden,
     bias, cum, cum_t, state_out, state_in, prior_out, prior,
     w_sem, kv_send, kv_recv, tok_send, tok_recv, rs_send, s1_sem, s2_sem, f1_sem, f2_sem, z_sem,
     go_send, go_recv, back_send, back_recv, st_send, st_recv, pr_send, pr_recv,
@@ -135,6 +158,12 @@
     kv_first, kv_arrive = gather(kv, SEQ, kv_send, kv_recv)
     tok_first, tok_arrive = gather(tok, ROWS, tok_send, tok_recv)
 
+    wide[...] = sum(
+        taken.astype(F32) * moe_in[r : r + 1, :].astype(F32) for r, (_, taken) in enumerate(slots_of(routes))
+    )
+    for i in range(EXPERTS):
+        slabs[i] = wide[2 * i : 2 * i + 2, :].astype(BF16)
+
     @pl.loop(1, EXPERTS)
     def _(k):
         to = (e + k) % EXPERTS
@@ -156,7 +185,7 @@
         low = (a - high.astype(F32) - mid.astype(F32)).astype(BF16)
         return high, mid, low
 
-    cum[...] = sum(dot(lower, term) for term in three(decay[...]))
+    cum[...] = sum(dot(lower, term, ((1,), (1,))) for term in three(decay_t[...]))
     cum_t[...] = sum(dot(term, lower, ((1,), (1,))) for term in three(decay_t[...]))
     last = cum[SEQ - 1 : SEQ, :]
     line = lax.broadcasted_iota(jnp.int32, (16, HEAD), 0)
@@ -275,7 +304,10 @@
         def add(k, sums):
             at = pl.ds(pl.multiple_of(k * chunk, chunk), chunk)
             tokens = tok[group(ds), at]
-            return sums[0] + dot(tokens, gate[at, :]), sums[1] + dot(tokens, up[at, :])
+            return (
+                sums[0] + dot(tokens, gate[:, at], ((1,), (1,))),
+                sums[1] + dot(tokens, up[:, at], ((1,), (1,))),
+            )
 
         zero = jnp.zeros((8 * ROWS, FF), F32)
         a, b = lax.fori_loop(0, D // chunk, add, (zero, zero))
@@ -421,26 +453,17 @@
     soft_query,
     soft_kv,
 ):
-    rows = moe_input.shape[0]
-    pairs = rows * TOP
-    flat = routes.reshape(pairs)
-    order = jnp.arange(pairs, dtype=jnp.int32)
-    rank = jnp.sum((flat[:, None] == flat[None, :]) & (order[None, :] < order[:, None]), axis=1)
-    slot = (flat * CAP + rank).reshape(rows, TOP)
-    chosen = slot[None] == jnp.arange(CAP * EXPERTS, dtype=jnp.int32)[:, None, None]
-    pick = jnp.any(chosen, axis=2).astype(BF16)
-    slabs = jnp.dot(pick, moe_input, preferred_element_type=F32).astype(BF16).reshape(EXPERTS, CAP, D)
-
     vmem, any_ = pl.BlockSpec(memory_space=pltpu.VMEM), pl.BlockSpec(memory_space=pl.ANY)
+    smem = pl.BlockSpec(memory_space=pltpu.SMEM)
     dma = pltpu.SemaphoreType.DMA
-    ret, lin_out, soft_out = pl.pallas_call(
+    ret, lin, soft = pl.pallas_call(
         kernel,
         out_shape=(
             jax.ShapeDtypeStruct((EXPERTS, CAP, D), BF16),
             jax.ShapeDtypeStruct((SEQ, HEADS * HEAD), BF16),
             jax.ShapeDtypeStruct((SEQ, HEADS * HEAD), BF16),
         ),
-        in_specs=[vmem, vmem, any_, any_, any_] + [vmem] * 7,
+        in_specs=[smem, vmem, vmem, any_, any_, any_] + [vmem] * 6,
         out_specs=(vmem, vmem, vmem),
         scratch_shapes=[
             pltpu.VMEM((CTX * SEQ, 2 * HEAD), BF16),
@@ -453,9 +476,10 @@
             pltpu.VMEM((ROWS, D), BF16),
             pltpu.VMEM((EXPERTS, CAP, D), BF16),
             pltpu.VMEM((EXPERTS, CAP, D), BF16),
+            pltpu.VMEM((EXPERTS, CAP, D), BF16),
             pltpu.VMEM((ROWS, D), F32),
-            pltpu.VMEM((D, FF), BF16),
-            pltpu.VMEM((D, FF), BF16),
+            pltpu.VMEM((FF, D), BF16),
+            pltpu.VMEM((FF, D), BF16),
             pltpu.VMEM((FF, D), BF16),
             pltpu.VMEM((CTX * ROWS, FF), BF16),
             pltpu.VMEM((SEQ, CTX * SEQ), F32),
@@ -475,23 +499,30 @@
             collective_id=0, has_side_effects=True, vmem_limit_bytes=58 * 2**20
         ),
     )(
-        slabs,
+        routes.T,
+        moe_input,
         soft_kv.reshape(SEQ, 2 * HEAD),
-        gate_weight.reshape(D, FF),
-        up_weight.reshape(D, FF),
+        gate_weight.reshape(D, FF).T,
+        up_weight.reshape(D, FF).T,
         down_weight.reshape(FF, D),
         lin_query,
         lin_key,
         lin_value,
-        log_decay,
         log_decay.T,
         lin_gain.reshape(1, HEADS * HEAD),
         soft_query,
     )
-    mix = jnp.sum(jnp.where(chosen, route_weight[None], 0.0), axis=2)
-    moe_out = lax.dot_general(
-        mix, ret.reshape(CAP * EXPERTS, D).astype(F32), (((0,), (0,)), ((), ())), precision=lax.Precision.HIGHEST
-    ).astype(BF16)
+    lin_out, moe_out, soft_out = pl.pallas_call(
+        finish,
+        out_shape=(
+            jax.ShapeDtypeStruct((SEQ, HEADS * HEAD), BF16),
+            jax.ShapeDtypeStruct(moe_input.shape, BF16),
+            jax.ShapeDtypeStruct((SEQ, HEADS * HEAD), BF16),
+        ),
+        in_specs=[smem, smem, vmem, vmem, vmem],
+        out_specs=(vmem, vmem, vmem),
+        scratch_shapes=[pltpu.VMEM((ROWS, D), F32)],
+    )(routes.T, route_weight.T, ret, lin, soft)
     return (lin_out, moe_out, soft_out)
 
 

time: 155 us -> 138 us (0.89)
  local copies, waits for them, and re-layouts: 22.4 us -> 1.48 us
  Pallas kernels: 130 us -> 136 us
    unnamed x10 -> x1, local copies, waits for them, and re-layouts: 20.4 us -> 1.48 us
    pallas_call x1, Pallas kernels: 130 us -> 134 us  [on_device(): pl.pallas_call(kernel, out_shape=(jax.ShapeDtypeStruct((EXPERTS, CAP, D),...]
    pallas_call x0 -> x1, Pallas kernels: none -> 2.49 us  [on_device(): pl.pallas_call(finish, out_shape=(jax.ShapeDtypeStruct((SEQ, HEADS * HEAD...]
    reshape x2 -> x0, local copies, waits for them, and re-layouts: 1.83 us -> none  [the longest x1 1 us: on_device(): ret.reshape(CAP * EXPERTS, D).astype(F32)]
where the time goes in v2:
time: 138 us
  Pallas kernels  136 us (99%)
  local copies, waits for them, and re-layouts  1.48 us (1%)
    pallas_call x1, Pallas kernels, on_device(): pl.pallas_call(kernel, out_shape=(jax.ShapeDtypeStruct((EXPERTS, CAP, D),...  134 us

profile of v2, /device:TPU:1, one launch (start us, length us, event | category | flops | bytes accessed | tf_op | source)
XLA Modules:
  0.0 138.2 jit_solution(5697856760537660621)
XLA Ops:
  0.6 1.5 %copy.18 = bf16[16,8,2,128]{3,1,2,0:T(8,128)(2,1)} copy(bf16[16,8,2,128]{3,2,1,0:T(2,128)(2,1)} %bitcast.20) | data formatting | bytes 131072
  2.1 133.5 %shard_map.148 = (bf16[8,2,6144]{2,1,0:T(2,128)(2,1)}, bf16[128,1024]{1,0:T(8,128)(2,1)}, bf16[128,1024]{1,0:T(8,128)(2,1)}) custom-call(s32[2,6]{1,0:T(2,128)} %bitcast.23, bf16[6,6144]{1,0:T(8,128)(2,1)} %moe_in.1, bf16[128,256]{1,0:T(8,128)(2,1)} %bitcast.19, bf16[288,6144]{1,0:T(8,128)(2,1)} %bitcast.16, bf16[288,6144]{1,0:T(8,128)(2,1)} %bitcast.17, ...), custom_call_target="tpu_custom_call" | custom-call | tf_op jit(solution)/shard_map/pallas_call | solution.py:459
  135.7 2.5 %shard_map.149 = (bf16[128,1024]{1,0:T(8,128)(2,1)}, bf16[6,6144]{1,0:T(8,128)(2,1)}, bf16[128,1024]{1,0:T(8,128)(2,1)}) custom-call(s32[2,6]{1,0:T(2,128)} %bitcast.24, f32[2,6]{1,0:T(2,128)} %bitcast.25, bf16[8,2,6144]{2,1,0:T(2,128)(2,1)} %get-tuple-element.6.ret, bf16[128,1024]{1,0:T(8,128)(2,1)} %get-tuple-element.7.lin, ...), custom_call_target="tpu_custom_call" | custom-call | tf_op jit(solution)/shard_map/pallas_call | solution.py:515

commit v3 on v2

--- a/solution.py
+++ b/solution.py
@@ -155,7 +155,44 @@
 
         return own, arrive
 
-    kv_first, kv_arrive = gather(kv, SEQ, kv_send, kv_recv)
+    kv_used = [0]
+
+    def kv_put(step, to, half=None):
+        where = rows_of(step, SEQ)
+        if half is not None:
+            where = pl.ds(pl.multiple_of(index_of(step) * SEQ + half * (SEQ // 2), SEQ // 2), SEQ // 2)
+        sem = kv_recv.at[2 * index_of(step) + (half or 0)]
+        push(kv.at[where], kv.at[where], kv_send.at[kv_used[0]], sem, (ctx_of(to), e))
+        kv_used[0] += 1
+
+    def kv_arrive(*steps):
+        for ds, df, dz in steps:
+            at = index_of((ds, df, dz))
+            if dz == 0 and (ds == 2 or (ds == 0 and df == 2)):
+                for half in (0, 1):
+                    where = pl.ds(pl.multiple_of(at * SEQ + half * (SEQ // 2), SEQ // 2), SEQ // 2)
+                    landed(kv.at[where], kv_recv.at[2 * at + half], kv_send.at[0])
+            elif (ds, df, dz) != (0, 0, 0):
+                landed(kv.at[rows_of((ds, df, dz), SEQ)], kv_recv.at[2 * at], kv_send.at[0])
+            if dz == 1:
+                continue
+            step = (ds, df, 0)
+            if ds == 0:
+                if df == 0:
+                    kv_put(step, (0, 1, 0))
+                    kv_put(step, (0, -1, 0))
+                elif df == -1:
+                    kv_put(step, (0, 1, 0), 0)
+                elif df == 1:
+                    kv_put(step, (0, -1, 0), 1)
+                kv_put(step, (1, 0, 0))
+                kv_put(step, (-1, 0, 0))
+            elif ds == -1:
+                kv_put(step, (1, 0, 0), 0)
+            elif ds == 1:
+                kv_put(step, (-1, 0, 0), 1)
+            kv_put(step, (0, 0, 1))
+
     tok_first, tok_arrive = gather(tok, ROWS, tok_send, tok_recv)
 
     wide[...] = sum(
@@ -173,7 +210,7 @@
         ).start()
 
     kv[rows_of((0, 0, 0), SEQ), :] = kv_own[...]
-    kv_first()
+    kv_arrive((0, 0, 0))
 
     row = lax.broadcasted_iota(jnp.int32, (SEQ, SEQ), 0)
     col = lax.broadcasted_iota(jnp.int32, (SEQ, SEQ), 1)
@@ -210,7 +247,7 @@
 
     state_in[c] = state_out[c]
 
-    kv_arrive((0, 0, 1), (0, 1, 0), (0, -1, 0), (1, 0, 0), (-1, 0, 0))
+    kv_arrive((0, 1, 0), (0, -1, 0))
 
     got[e] = slabs[e]
 
@@ -226,39 +263,6 @@
         wide[2 * i : 2 * i + 2, :] = got[i].astype(F32)
     tok[rows_of((0, 0, 0), ROWS), :] = wide[...].astype(BF16)
     tok_first()
-
-    kv_arrive((0, 1, 1), (0, -1, 1), (1, 0, 1), (-1, 0, 1), (0, 2, 0), (0, 2, 1))
-    kv_arrive(*((ds, df, 0) for df in (1, -1) for ds in (1, -1)))
-    tok_arrive((0, 0, 1), (0, 1, 0), (0, -1, 0), (1, 0, 0), (-1, 0, 0))
-    kv_arrive(*((ds, df, 1) for df in (1, -1) for ds in (1, -1)))
-    kv_arrive(*((ds, 2, dz) for dz in (0, 1) for ds in (1, -1)))
-    kv_arrive(*((2, df, dz) for df in (0, 1, -1, 2) for dz in (0, 1)))
-    tok_arrive((0, 1, 1), (0, -1, 1))
-
-    @pl.loop(1, CTX)
-    def _(k):
-        at = (c + k) % CTX
-        pltpu.make_async_remote_copy(
-            src_ref=state_out.at[at], dst_ref=state_in.at[at], send_sem=st_send.at[at], recv_sem=st_recv.at[at],
-            device_id=(at, e), device_id_type=MESH,
-        ).wait()
-
-    def hop(i, run):
-        prior_out[i] = run.astype(BF16)
-        logs = jnp.sum(state_in[i, 32:48, :].astype(F32), axis=0, keepdims=True)
-        return jnp.exp(logs) * run + state_in[i, 0:32, :].astype(F32)
-
-    lax.fori_loop(0, CTX, hop, jnp.zeros((32, HEAD), F32))
-
-    @pl.loop(1, CTX)
-    def _(k):
-        to = (c + k) % CTX
-        pltpu.make_async_remote_copy(
-            src_ref=prior_out.at[to], dst_ref=prior.at[c], send_sem=pr_send.at[to], recv_sem=pr_recv.at[c],
-            device_id=(to, e), device_id_type=MESH,
-        ).start()
-
-    prior[c] = prior_out[c]
 
     wide_col = lax.broadcasted_iota(jnp.int32, (8, CTX * SEQ), 1)
     blk = jnp.right_shift(wide_col, 7)
@@ -319,21 +323,53 @@
             at = pl.ds(pl.multiple_of(k * chunk, chunk), chunk)
             part[group(ds), at] = dot(hidden[group(ds), :], down[:, at]).astype(BF16)
 
-    attend(0, 1)
-    tok_arrive((1, 0, 1), (-1, 0, 1), (0, 2, 0), (0, 2, 1))
-    attend(1, 1)
-    tok_arrive(*((ds, df, 0) for df in (1, -1) for ds in (1, -1)))
-    attend(2, 1)
-    attend(3, 1)
-    tok_arrive(*((ds, df, 1) for df in (1, -1) for ds in (1, -1)))
-    attend(4, 2)
+    def pairs(df, dz):
+        return (1, df, dz), (-1, df, dz)
+
+    kv_arrive(*pairs(0, 0), (0, 2, 0))
+    tok_arrive((0, 0, 1), (0, 1, 0), (0, -1, 0))
+    kv_arrive(*pairs(1, 0), *pairs(-1, 0))
+    tok_arrive(*pairs(0, 0))
+    kv_arrive(*pairs(2, 0))
+    tok_arrive((0, 1, 1), (0, -1, 1))
+    kv_arrive((2, 0, 0), (2, 1, 0))
+    tok_arrive(*pairs(0, 1), (0, 2, 0), (0, 2, 1))
+    kv_arrive((2, -1, 0), (2, 2, 0))
+    tok_arrive(*pairs(1, 0), *pairs(-1, 0))
+    tok_arrive(*pairs(1, 1), *pairs(-1, 1))
     for copy in weights:
         copy.wait()
     enter(0)
-    tok_arrive(*((ds, 2, dz) for dz in (0, 1) for ds in (1, -1)))
-    attend(6, 2)
+    tok_arrive(*pairs(2, 0), *pairs(2, 1))
     enter(1)
     enter(-1)
+    kv_arrive(*((ds, df, 1) for ds in (0, 1, -1, 2) for df in (0, 1, -1, 2)))
+
+    @pl.loop(1, CTX)
+    def _(k):
+        at = (c + k) % CTX
+        pltpu.make_async_remote_copy(
+            src_ref=state_out.at[at], dst_ref=state_in.at[at], send_sem=st_send.at[at], recv_sem=st_recv.at[at],
+            device_id=(at, e), device_id_type=MESH,
+        ).wait()
+
+    def hop(i, run):
+        prior_out[i] = run.astype(BF16)
+        logs = jnp.sum(state_in[i, 32:48, :].astype(F32), axis=0, keepdims=True)
+        return jnp.exp(logs) * run + state_in[i, 0:32, :].astype(F32)
+
+    lax.fori_loop(0, CTX, hop, jnp.zeros((32, HEAD), F32))
+
+    @pl.loop(1, CTX)
+    def _(k):
+        to = (c + k) % CTX
+        pltpu.make_async_remote_copy(
+            src_ref=prior_out.at[to], dst_ref=prior.at[c], send_sem=pr_send.at[to], recv_sem=pr_recv.at[c],
+            device_id=(to, e), device_id_type=MESH,
+        ).start()
+
+    prior[c] = prior_out[c]
+
     tok_arrive(*((2, df, dz) for df in (0, 1, -1, 2) for dz in (0, 1)))
     enter(2)
 
@@ -365,21 +401,23 @@
         send_part((1, df, 0), block(s2r, 4 * i + 2), s2_sem.at[4 * i + 2], (1, 0, 0))
     leave(0)
 
-    @pl.loop(1, CTX)
-    def _(k):
-        at = (c + k) % CTX
-        pltpu.make_async_remote_copy(
-            src_ref=prior_out.at[at], dst_ref=prior.at[at], send_sem=pr_send.at[at], recv_sem=pr_recv.at[at],
-            device_id=(at, e), device_id_type=MESH,
-        ).wait()
-
     for i, df in enumerate(DFS):
         for k, step, to in ((0, (-1, df, 0), (-1, 0, 0)), (1, (1, df, 1), (1, 0, 0))):
             landed(block(s1r, 2 * i + k), s1_sem.at[2 * i + k], rs_send.at[0])
             add_in(step, block(s1r, 2 * i + k))
             slot = 4 * i + (0 if k == 0 else 3)
             send_part(step, block(s2r, slot), s2_sem.at[slot], to)
-        finish_lightning((2 * i, 2 * i + 1))
+        attend(2 * i, 2)
+
+    @pl.loop(1, CTX)
+    def _(k):
+        at = (c + k) % CTX
+        pltpu.make_async_remote_copy(
+            src_ref=prior_out.at[at], dst_ref=prior.at[at], send_sem=pr_send.at[at], recv_sem=pr_recv.at[at],
+            device_id=(at, e), device_id_type=MESH,
+        ).wait()
+
+    finish_lightning(range(HEADS))
 
     for i, df in enumerate(DFS):
         for slot in (1, 2, 0, 3):
@@ -490,7 +528,7 @@
             pltpu.VMEM((CTX, 32, HEAD), BF16),
             pltpu.VMEM((CTX, 32, HEAD), BF16),
             dma((3,)),
-            dma((31,)), dma((32,)), dma((31,)), dma((32,)), dma((31,)),
+            dma((36,)), dma((64,)), dma((31,)), dma((32,)), dma((31,)),
             dma((8,)), dma((16,)), dma((2,)), dma((4,)), dma((1,)),
             dma((EXPERTS,)), dma((EXPERTS,)), dma((EXPERTS,)), dma((EXPERTS,)),
             dma((CTX,)), dma((CTX,)), dma((CTX,)), dma((CTX,)),

time: 138 us -> 126 us (0.913)
  Pallas kernels: 136 us -> 124 us
    pallas_call x1, Pallas kernels: 134 us -> 121 us  [on_device(): pl.pallas_call(kernel, out_shape=(jax.ShapeDtypeStruct((EXPERTS, CAP, D),...]
where the time goes in v3:
time: 126 us
  Pallas kernels  124 us (98%)
  local copies, waits for them, and re-layouts  1.48 us (1%)
    pallas_call x1, Pallas kernels, on_device(): pl.pallas_call(kernel, out_shape=(jax.ShapeDtypeStruct((EXPERTS, CAP, D),...  121 us

profile of v3, /device:TPU:1, one launch (start us, length us, event | category | flops | bytes accessed | tf_op | source)
XLA Modules:
  0.0 125.7 jit_solution(1051459617047060269)
XLA Ops:
  0.6 1.5 %copy.18 = bf16[16,8,2,128]{3,1,2,0:T(8,128)(2,1)} copy(bf16[16,8,2,128]{3,2,1,0:T(2,128)(2,1)} %bitcast.20) | data formatting | bytes 131072
  2.1 121.1 %shard_map.148 = (bf16[8,2,6144]{2,1,0:T(2,128)(2,1)}, bf16[128,1024]{1,0:T(8,128)(2,1)}, bf16[128,1024]{1,0:T(8,128)(2,1)}) custom-call(s32[2,6]{1,0:T(2,128)} %bitcast.23, bf16[6,6144]{1,0:T(8,128)(2,1)} %moe_in.1, bf16[128,256]{1,0:T(8,128)(2,1)} %bitcast.19, bf16[288,6144]{1,0:T(8,128)(2,1)} %bitcast.16, bf16[288,6144]{1,0:T(8,128)(2,1)} %bitcast.17, ...), custom_call_target="tpu_custom_call" | custom-call | tf_op jit(solution)/shard_map/pallas_call | solution.py:497
  123.2 2.5 %shard_map.149 = (bf16[128,1024]{1,0:T(8,128)(2,1)}, bf16[6,6144]{1,0:T(8,128)(2,1)}, bf16[128,1024]{1,0:T(8,128)(2,1)}) custom-call(s32[2,6]{1,0:T(2,128)} %bitcast.24, f32[2,6]{1,0:T(2,128)} %bitcast.25, bf16[8,2,6144]{2,1,0:T(2,128)(2,1)} %get-tuple-element.6.ret, bf16[128,1024]{1,0:T(8,128)(2,1)} %get-tuple-element.7.lin, ...), custom_call_target="tpu_custom_call" | custom-call | tf_op jit(solution)/shard_map/pallas_call | solution.py:553

commit v4 on v3

--- a/solution.py
+++ b/solution.py
@@ -21,6 +21,7 @@
 F32, BF16 = jnp.float32, jnp.bfloat16
 MESH = pl.DeviceIdType.MESH
 DFS = (2, 1, -1, 0)
+MAIN, SIDE = 4096, 1024
 
 
 def dot(a, b, dims=((1,), (0,))):
@@ -59,7 +60,7 @@
 def kernel(
     routes, moe_in, kv_own, gate_hbm, up_hbm, down_hbm, lin_q, lin_k, lin_v, decay_t, gain, soft_q,
     ret, lin_out, soft_out,
-    kv, tok, part, s1r, s2r, f1r, f2r, zr, slabs, got, back, wide, gate, up, down, hidden,
+    kv, tok, part, s1r, s2r, f1r, f2r, zr, zt, slabs, got, back, wide, gate, up, down, hidden,
     bias, cum, cum_t, state_out, state_in, prior_out, prior,
     w_sem, kv_send, kv_recv, tok_send, tok_recv, rs_send, s1_sem, s2_sem, f1_sem, f2_sem, z_sem,
     go_send, go_recv, back_send, back_recv, st_send, st_recv, pr_send, pr_recv,
@@ -102,14 +103,10 @@
     for copy in weights:
         copy.start()
 
-    unfinished = []
-
     def push(src, dst, send_sem, recv_sem, to):
-        copy = pltpu.make_async_remote_copy(
+        pltpu.make_async_remote_copy(
             src_ref=src, dst_ref=dst, send_sem=send_sem, recv_sem=recv_sem, device_id=to, device_id_type=MESH
-        )
-        copy.start()
-        unfinished.append(copy)
+        ).start()
 
     def landed(ref, recv_sem, spare_sem):
         pltpu.make_async_remote_copy(
@@ -117,13 +114,16 @@
             device_id=(ctx_of((0, 0, 1)), e), device_id_type=MESH,
         ).wait_recv()
 
+    def all_of(ref, send_sem, recv_sem):
+        return pltpu.make_async_remote_copy(
+            src_ref=ref, dst_ref=ref, send_sem=send_sem, recv_sem=recv_sem,
+            device_id=(ctx_of((0, 0, 1)), e), device_id_type=MESH,
+        )
+
     def gather(buf, rows, send_sems, recv_sems):
-        used = [0]
-
         def send(step, to):
             where = rows_of(step, rows)
-            push(buf.at[where], buf.at[where], send_sems.at[used[0]], recv_sems.at[index_of(step)], (ctx_of(to), e))
-            used[0] += 1
+            push(buf.at[where], buf.at[where], send_sems.at[0], recv_sems.at[index_of(step)], (ctx_of(to), e))
 
         def sideways(step):
             send(step, (1, 0, 0))
@@ -155,15 +155,12 @@
 
         return own, arrive
 
-    kv_used = [0]
-
     def kv_put(step, to, half=None):
         where = rows_of(step, SEQ)
         if half is not None:
             where = pl.ds(pl.multiple_of(index_of(step) * SEQ + half * (SEQ // 2), SEQ // 2), SEQ // 2)
-        sem = kv_recv.at[2 * index_of(step) + (half or 0)]
-        push(kv.at[where], kv.at[where], kv_send.at[kv_used[0]], sem, (ctx_of(to), e))
-        kv_used[0] += 1
+        sem = kv_recv.at[2 * CTX if to == (0, 0, 1) else 2 * index_of(step) + (half or 0)]
+        push(kv.at[where], kv.at[where], kv_send.at[0], sem, (ctx_of(to), e))
 
     def kv_arrive(*steps):
         for ds, df, dz in steps:
@@ -174,8 +171,6 @@
                     landed(kv.at[where], kv_recv.at[2 * at + half], kv_send.at[0])
             elif (ds, df, dz) != (0, 0, 0):
                 landed(kv.at[rows_of((ds, df, dz), SEQ)], kv_recv.at[2 * at], kv_send.at[0])
-            if dz == 1:
-                continue
             step = (ds, df, 0)
             if ds == 0:
                 if df == 0:
@@ -205,11 +200,12 @@
     def _(k):
         to = (e + k) % EXPERTS
         pltpu.make_async_remote_copy(
-            src_ref=slabs.at[to], dst_ref=got.at[e], send_sem=go_send.at[to], recv_sem=go_recv.at[e],
+            src_ref=slabs.at[to], dst_ref=got.at[e], send_sem=go_send.at[0], recv_sem=go_recv.at[0],
             device_id=(c, to), device_id_type=MESH,
         ).start()
 
-    kv[rows_of((0, 0, 0), SEQ), :] = kv_own[...]
+    for i in (0, 1):
+        kv[rows_of((0, 0, 0), SEQ), i * HEAD : (i + 1) * HEAD] = kv_own[:, i, :]
     kv_arrive((0, 0, 0))
 
     row = lax.broadcasted_iota(jnp.int32, (SEQ, SEQ), 0)
@@ -241,7 +237,7 @@
     def _(k):
         to = (c + k) % CTX
         pltpu.make_async_remote_copy(
-            src_ref=state_out.at[to], dst_ref=state_in.at[c], send_sem=st_send.at[to], recv_sem=st_recv.at[c],
+            src_ref=state_out.at[to], dst_ref=state_in.at[c], send_sem=st_send.at[0], recv_sem=st_recv.at[0],
             device_id=(to, e), device_id_type=MESH,
         ).start()
 
@@ -251,13 +247,7 @@
 
     got[e] = slabs[e]
 
-    @pl.loop(1, EXPERTS)
-    def _(k):
-        at = (e + k) % EXPERTS
-        pltpu.make_async_remote_copy(
-            src_ref=slabs.at[at], dst_ref=got.at[at], send_sem=go_send.at[at], recv_sem=go_recv.at[at],
-            device_id=(c, at), device_id_type=MESH,
-        ).wait()
+    all_of(got.at[pl.ds(0, EXPERTS - 1)], go_send.at[0], go_recv.at[0]).wait()
 
     for i in range(EXPERTS):
         wide[2 * i : 2 * i + 2, :] = got[i].astype(F32)
@@ -343,15 +333,9 @@
     tok_arrive(*pairs(2, 0), *pairs(2, 1))
     enter(1)
     enter(-1)
-    kv_arrive(*((ds, df, 1) for ds in (0, 1, -1, 2) for df in (0, 1, -1, 2)))
-
-    @pl.loop(1, CTX)
-    def _(k):
-        at = (c + k) % CTX
-        pltpu.make_async_remote_copy(
-            src_ref=state_out.at[at], dst_ref=state_in.at[at], send_sem=st_send.at[at], recv_sem=st_recv.at[at],
-            device_id=(at, e), device_id_type=MESH,
-        ).wait()
+    landed(kv.at[pl.ds(0, CTX // 2 * SEQ)], kv_recv.at[2 * CTX], kv_send.at[0])
+
+    all_of(state_in.at[pl.ds(0, CTX - 1)], st_send.at[0], st_recv.at[0]).wait()
 
     def hop(i, run):
         prior_out[i] = run.astype(BF16)
@@ -364,7 +348,7 @@
     def _(k):
         to = (c + k) % CTX
         pltpu.make_async_remote_copy(
-            src_ref=prior_out.at[to], dst_ref=prior.at[c], send_sem=pr_send.at[to], recv_sem=pr_recv.at[c],
+            src_ref=prior_out.at[to], dst_ref=prior.at[c], send_sem=pr_send.at[0], recv_sem=pr_recv.at[0],
             device_id=(to, e), device_id_type=MESH,
         ).start()
 
@@ -373,83 +357,129 @@
     tok_arrive(*((2, df, dz) for df in (0, 1, -1, 2) for dz in (0, 1)))
     enter(2)
 
-    rs_used = [0]
-
-    def send_part(step, dst, sem, to):
-        push(part.at[rows_of(step, ROWS)], dst, rs_send.at[rs_used[0]], sem, (ctx_of(to), e))
-        rs_used[0] += 1
-
-    def block(ref, i):
-        return ref.at[pl.ds(i * ROWS, ROWS)]
-
-    def add_in(step, *blocks):
-        where = rows_of(step, ROWS)
-        total = part[where, :].astype(F32)
+    numbered = tuple(enumerate(DFS))
+
+    def put(src, dst, kind, sem, to):
+        push(src, dst, rs_send.at[kind], sem, (ctx_of(to), e))
+
+    def piece(side, step):
+        ds, df, unit = step
+        if side:
+            return part.at[rows_of((ds, df, 0), ROWS), pl.ds(MAIN + SIDE * unit, SIDE)]
+        return part.at[rows_of(step, ROWS), pl.ds(0, MAIN)]
+
+    def block(ref, side, i):
+        return ref.at[pl.ds(i * ROWS, ROWS), pl.ds(MAIN, SIDE) if side else pl.ds(0, MAIN)]
+
+    def add_in(ref, *blocks):
+        total = ref[...].astype(F32)
         for b in blocks:
             total = total + b[...].astype(F32)
-        part[where, :] = total.astype(BF16)
+        ref[...] = total.astype(BF16)
+
+    def take(ref, sems, side, count, i):
+        landed(block(ref, side, i), sems.at[side * count + i], rs_send.at[0])
+        return block(ref, side, i)
+
+    def over(side, step, ref, sems, count, i, to):
+        put(piece(side, step), block(ref, side, i), side, sems.at[side * count + i], to)
+
+    def z_rest(i):
+        return zt.at[pl.ds(i * ROWS, ROWS)]
+
+    def z_send(ds):
+        for i, df in numbered:
+            at = 4 * DFS.index(ds) + i
+            src = part.at[rows_of((ds, df, 1), ROWS), pl.ds(MAIN, 2 * SIDE)]
+            put(src, z_rest(at), 2, z_sem.at[1 + at], (0, 0, 1))
+
+    def z_add(ds, df):
+        at = 4 * DFS.index(ds) + DFS.index(df)
+        landed(z_rest(at), z_sem.at[1 + at], rs_send.at[0])
+        add_in(part.at[rows_of((ds, df, 0), ROWS), pl.ds(MAIN, 2 * SIDE)], z_rest(at))
+
+    def first(side, i, df):
+        over(side, (2, df, 0), s1r, s1_sem, 8, 2 * i, (-1, 0, 0))
+        over(side, (2, df, 1), s1r, s1_sem, 8, 2 * i + 1, (1, 0, 0))
+
+    def own_minus(side, i, df):
+        over(side, (-1, df, 1), s2r, s2_sem, 16, 4 * i + 1, (-1, 0, 0))
+
+    def own_plus(side, i, df):
+        over(side, (1, df, 0), s2r, s2_sem, 16, 4 * i + 2, (1, 0, 0))
+
+    def forward(side, i, df):
+        for unit, ds in ((0, -1), (1, 1)):
+            add_in(piece(side, (ds, df, unit)), take(s1r, s1_sem, side, 8, 2 * i + unit))
+            over(side, (ds, df, unit), s2r, s2_sem, 16, 4 * i + 3 * unit, (ds, 0, 0))
+
+    def settle(side, i, df):
+        got_s = [take(s2r, s2_sem, side, 16, 4 * i + k) for k in (1, 2, 0, 3)]
+        add_in(piece(side, (0, df, 0)), got_s[2], got_s[1])
+        add_in(piece(side, (0, df, 1)), got_s[0], got_s[3])
+        if df == 2:
+            over(side, (0, 2, 0), f1r, f1_sem, 2, 0, (0, -1, 0))
+            over(side, (0, 2, 1), f1r, f1_sem, 2, 1, (0, 1, 0))
+        elif df == 1:
+            over(side, (0, 1, 0), f2r, f2_sem, 4, 2, (0, 1, 0))
+        elif df == -1:
+            over(side, (0, -1, 1), f2r, f2_sem, 4, 1, (0, -1, 0))
+            for unit, way in ((0, -1), (1, 1)):
+                add_in(piece(side, (0, way, unit)), take(f1r, f1_sem, side, 2, unit))
+                over(side, (0, way, unit), f2r, f2_sem, 4, 3 * unit, (0, way, 0))
+
+    def total(side, unit):
+        here = [take(f2r, f2_sem, side, 4, k) for k in (unit, 2 + unit)]
+        return piece(side, (0, 0, unit))[...].astype(F32) + here[0][...].astype(F32) + here[1][...].astype(F32)
 
     leave(2)
-    for i, df in enumerate(DFS):
-        send_part((2, df, 0), block(s1r, 2 * i), s1_sem.at[2 * i], (-1, 0, 0))
-        send_part((2, df, 1), block(s1r, 2 * i + 1), s1_sem.at[2 * i + 1], (1, 0, 0))
+    z_send(2)
+    for i, df in numbered:
+        first(0, i, df)
     leave(-1)
-    for i, df in enumerate(DFS):
-        send_part((-1, df, 1), block(s2r, 4 * i + 1), s2_sem.at[4 * i + 1], (-1, 0, 0))
+    z_send(-1)
+    for i, df in numbered:
+        own_minus(0, i, df)
     leave(1)
-    for i, df in enumerate(DFS):
-        send_part((1, df, 0), block(s2r, 4 * i + 2), s2_sem.at[4 * i + 2], (1, 0, 0))
+    z_send(1)
+    for i, df in numbered:
+        own_plus(0, i, df)
     leave(0)
-
-    for i, df in enumerate(DFS):
-        for k, step, to in ((0, (-1, df, 0), (-1, 0, 0)), (1, (1, df, 1), (1, 0, 0))):
-            landed(block(s1r, 2 * i + k), s1_sem.at[2 * i + k], rs_send.at[0])
-            add_in(step, block(s1r, 2 * i + k))
-            slot = 4 * i + (0 if k == 0 else 3)
-            send_part(step, block(s2r, slot), s2_sem.at[slot], to)
+    z_send(0)
+
+    all_of(prior.at[pl.ds(0, CTX - 1)], pr_send.at[0], pr_recv.at[0]).wait()
+
+    for i, df in numbered:
+        forward(0, i, df)
+        z_add(2, df)
+        first(1, i, df)
         attend(2 * i, 2)
-
-    @pl.loop(1, CTX)
-    def _(k):
-        at = (c + k) % CTX
-        pltpu.make_async_remote_copy(
-            src_ref=prior_out.at[at], dst_ref=prior.at[at], send_sem=pr_send.at[at], recv_sem=pr_recv.at[at],
-            device_id=(at, e), device_id_type=MESH,
-        ).wait()
-
-    finish_lightning(range(HEADS))
-
-    for i, df in enumerate(DFS):
-        for slot in (1, 2, 0, 3):
-            landed(block(s2r, 4 * i + slot), s2_sem.at[4 * i + slot], rs_send.at[0])
-        add_in((0, df, 0), block(s2r, 4 * i), block(s2r, 4 * i + 2))
-        add_in((0, df, 1), block(s2r, 4 * i + 1), block(s2r, 4 * i + 3))
-        if df == 2:
-            send_part((0, 2, 0), block(f1r, 0), f1_sem.at[0], (0, -1, 0))
-            send_part((0, 2, 1), block(f1r, 1), f1_sem.at[1], (0, 1, 0))
-        elif df == 1:
-            send_part((0, 1, 0), block(f2r, 2), f2_sem.at[2], (0, 1, 0))
-        elif df == -1:
-            send_part((0, -1, 1), block(f2r, 1), f2_sem.at[1], (0, -1, 0))
-            for k, step, to in ((0, (0, -1, 0), (0, -1, 0)), (1, (0, 1, 1), (0, 1, 0))):
-                landed(block(f1r, k), f1_sem.at[k], rs_send.at[0])
-                add_in(step, block(f1r, k))
-                slot = 0 if k == 0 else 3
-                send_part(step, block(f2r, slot), f2_sem.at[slot], to)
-
-    landed(block(f2r, 1), f2_sem.at[1], rs_send.at[0])
-    landed(block(f2r, 3), f2_sem.at[3], rs_send.at[0])
-    add_in((0, 0, 1), block(f2r, 1), block(f2r, 3))
-    send_part((0, 0, 1), zr, z_sem.at[0], (0, 0, 1))
-    landed(block(f2r, 0), f2_sem.at[0], rs_send.at[0])
-    landed(block(f2r, 2), f2_sem.at[2], rs_send.at[0])
-    wide[...] = (
-        part[rows_of((0, 0, 0), ROWS), :].astype(F32)
-        + block(f2r, 0)[...].astype(F32)
-        + block(f2r, 2)[...].astype(F32)
-    )
+        finish_lightning((2 * i, 2 * i + 1))
+    settle(0, 0, 2)
+    for i, df in numbered:
+        z_add(-1, df)
+        own_minus(1, i, df)
+    settle(0, 1, 1)
+    for i, df in numbered:
+        z_add(1, df)
+        own_plus(1, i, df)
+        forward(1, i, df)
+    settle(0, 2, -1)
+    z_add(0, 2)
+    settle(1, 0, 2)
+    settle(0, 3, 0)
+    for i, df in numbered[1:3]:
+        z_add(0, df)
+        settle(1, i, df)
+    piece(0, (0, 0, 1))[...] = total(0, 1).astype(BF16)
+    put(piece(0, (0, 0, 1)), zr, 0, z_sem.at[0], (0, 0, 1))
+    wide[:, pl.ds(0, MAIN)] = total(0, 0)
+    z_add(0, 0)
+    settle(1, 3, 0)
+    for unit in (0, 1):
+        wide[:, pl.ds(MAIN + SIDE * unit, SIDE)] = total(1, unit)
     landed(zr, z_sem.at[0], rs_send.at[0])
-    wide[...] = wide[...] + zr[...].astype(F32)
+    wide[:, pl.ds(0, MAIN)] = wide[:, pl.ds(0, MAIN)] + zr[...].astype(F32)
 
     for i in range(EXPERTS):
         back[i] = wide[2 * i : 2 * i + 2, :].astype(BF16)
@@ -458,22 +488,19 @@
     def _(k):
         to = (e + k) % EXPERTS
         pltpu.make_async_remote_copy(
-            src_ref=back.at[to], dst_ref=ret.at[e], send_sem=back_send.at[to], recv_sem=back_recv.at[e],
+            src_ref=back.at[to], dst_ref=ret.at[e], send_sem=back_send.at[0], recv_sem=back_recv.at[0],
             device_id=(c, to), device_id_type=MESH,
         ).start()
 
     ret[e] = back[e]
 
-    @pl.loop(1, EXPERTS)
-    def _(k):
-        at = (e + k) % EXPERTS
-        pltpu.make_async_remote_copy(
-            src_ref=back.at[at], dst_ref=ret.at[at], send_sem=back_send.at[at], recv_sem=back_recv.at[at],
-            device_id=(c, at), device_id_type=MESH,
-        ).wait()
-
-    for copy in unfinished:
-        copy.wait_send()
+    all_of(back.at[pl.ds(0, EXPERTS - 1)], back_send.at[0], back_recv.at[0]).wait()
+
+    all_of(tok.at[pl.ds(0, 31 * ROWS)], tok_send.at[0], tok_recv.at[0]).wait_send()
+    all_of(kv.at[pl.ds(0, 26 * SEQ + 10 * SEQ // 2)], kv_send.at[0], kv_recv.at[0]).wait_send()
+    for kind, blocks, columns in ((0, 31, MAIN), (1, 30, SIDE), (2, 16, 2 * SIDE)):
+        sent = part.at[pl.ds(0, blocks * ROWS), pl.ds(0, columns)]
+        all_of(sent, rs_send.at[kind], z_sem.at[0]).wait_send()
 
 
 def on_device(
@@ -511,7 +538,8 @@
             pltpu.VMEM((16 * ROWS, D), BF16),
             pltpu.VMEM((2 * ROWS, D), BF16),
             pltpu.VMEM((4 * ROWS, D), BF16),
-            pltpu.VMEM((ROWS, D), BF16),
+            pltpu.VMEM((ROWS, MAIN), BF16),
+            pltpu.VMEM((16 * ROWS, 2 * SIDE), BF16),
             pltpu.VMEM((EXPERTS, CAP, D), BF16),
             pltpu.VMEM((EXPERTS, CAP, D), BF16),
             pltpu.VMEM((EXPERTS, CAP, D), BF16),
@@ -528,10 +556,10 @@
             pltpu.VMEM((CTX, 32, HEAD), BF16),
             pltpu.VMEM((CTX, 32, HEAD), BF16),
             dma((3,)),
-            dma((36,)), dma((64,)), dma((31,)), dma((32,)), dma((31,)),
-            dma((8,)), dma((16,)), dma((2,)), dma((4,)), dma((1,)),
-            dma((EXPERTS,)), dma((EXPERTS,)), dma((EXPERTS,)), dma((EXPERTS,)),
-            dma((CTX,)), dma((CTX,)), dma((CTX,)), dma((CTX,)),
+            dma((1,)), dma((2 * CTX + 1,)), dma((1,)), dma((CTX,)), dma((3,)),
+            dma((16,)), dma((32,)), dma((4,)), dma((8,)), dma((17,)),
+            dma((1,)), dma((1,)), dma((1,)), dma((1,)),
+            dma((1,)), dma((1,)), dma((1,)), dma((1,)),
         ],
         compiler_params=pltpu.CompilerParams(
             collective_id=0, has_side_effects=True, vmem_limit_bytes=58 * 2**20
@@ -539,7 +567,7 @@
     )(
         routes.T,
         moe_input,
-        soft_kv.reshape(SEQ, 2 * HEAD),
+        soft_kv.reshape(SEQ, 2, HEAD),
         gate_weight.reshape(D, FF).T,
         up_weight.reshape(D, FF).T,
         down_weight.reshape(FF, D),

time: 126 us -> 116 us (0.921)
  Pallas kernels: 124 us -> 115 us
  local copies, waits for them, and re-layouts: 1.48 us -> 0 us
    pallas_call x1, Pallas kernels: 121 us -> 112 us  [on_device(): pl.pallas_call(kernel, out_shape=(jax.ShapeDtypeStruct((EXPERTS, CAP, D),...]
    unnamed x1 -> x0, local copies, waits for them, and re-layouts: 1.48 us -> none
where the time goes in v4:
time: 116 us
  Pallas kernels  115 us (99%)
    pallas_call x1, Pallas kernels, on_device(): pl.pallas_call(kernel, out_shape=(jax.ShapeDtypeStruct((EXPERTS, CAP, D),...  112 us
    pallas_call x1, Pallas kernels, on_device(): pl.pallas_call(finish, out_shape=(jax.ShapeDtypeStruct((SEQ, HEADS * HEAD...  2.49 us

profile of v4, /device:TPU:1, one launch (start us, length us, event | category | flops | bytes accessed | tf_op | source)
XLA Modules:
  0.0 115.6 jit_solution(12371982311515432131)
XLA Ops:
  0.6 112.5 %shard_map.148 = (bf16[8,2,6144]{2,1,0:T(2,128)(2,1)}, bf16[128,1024]{1,0:T(8,128)(2,1)}, bf16[128,1024]{1,0:T(8,128)(2,1)}) custom-call(s32[2,6]{1,0:T(2,128)} %bitcast.18, bf16[6,6144]{1,0:T(8,128)(2,1)} %moe_in.1, bf16[128,2,128]{2,1,0:T(2,128)(2,1)} %bitcast.15, bf16[288,6144]{1,0:T(8,128)(2,1)} %bitcast.12, bf16[288,6144]{1,0:T(8,128)(2,1)} %bitcast.13, ...), custom_call_target="tpu_custom_call" | custom-call | tf_op jit(solution)/shard_map/pallas_call | solution.py:524
  113.1 2.5 %shard_map.149 = (bf16[128,1024]{1,0:T(8,128)(2,1)}, bf16[6,6144]{1,0:T(8,128)(2,1)}, bf16[128,1024]{1,0:T(8,128)(2,1)}) custom-call(s32[2,6]{1,0:T(2,128)} %bitcast.19, f32[2,6]{1,0:T(2,128)} %bitcast.20, bf16[8,2,6144]{2,1,0:T(2,128)(2,1)} %get-tuple-element.6.ret, bf16[128,1024]{1,0:T(8,128)(2,1)} %get-tuple-element.7.lin, ...), custom_call_target="tpu_custom_call" | custom-call | tf_op jit(solution)/shard_map/pallas_call | solution.py:581

commit v5 on v4

--- a/solution.py
+++ b/solution.py
@@ -21,7 +21,7 @@
 F32, BF16 = jnp.float32, jnp.bfloat16
 MESH = pl.DeviceIdType.MESH
 DFS = (2, 1, -1, 0)
-MAIN, SIDE = 4096, 1024
+MAIN, SIDE = 3584, 1280
 
 
 def dot(a, b, dims=((1,), (0,))):
@@ -330,11 +330,6 @@
     for copy in weights:
         copy.wait()
     enter(0)
-    tok_arrive(*pairs(2, 0), *pairs(2, 1))
-    enter(1)
-    enter(-1)
-    landed(kv.at[pl.ds(0, CTX // 2 * SEQ)], kv_recv.at[2 * CTX], kv_send.at[0])
-
     all_of(state_in.at[pl.ds(0, CTX - 1)], st_send.at[0], st_recv.at[0]).wait()
 
     def hop(i, run):
@@ -353,6 +348,10 @@
         ).start()
 
     prior[c] = prior_out[c]
+    tok_arrive(*pairs(2, 0), *pairs(2, 1))
+    enter(1)
+    enter(-1)
+    landed(kv.at[pl.ds(0, CTX // 2 * SEQ)], kv_recv.at[2 * CTX], kv_send.at[0])
 
     tok_arrive(*((2, df, dz) for df in (0, 1, -1, 2) for dz in (0, 1)))
     enter(2)

time: 116 us -> 115 us (level)
  no operation moved by 1% of the time
where the time goes in v5:
time: 115 us
  Pallas kernels  114 us (99%)
    pallas_call x1, Pallas kernels, on_device(): pl.pallas_call(kernel, out_shape=(jax.ShapeDtypeStruct((EXPERTS, CAP, D),...  111 us
    pallas_call x1, Pallas kernels, on_device(): pl.pallas_call(finish, out_shape=(jax.ShapeDtypeStruct((SEQ, HEADS * HEAD...  2.49 us

profile of v5, /device:TPU:1, one launch (start us, length us, event | category | flops | bytes accessed | tf_op | source)
XLA Modules:
  0.0 114.5 jit_solution(17470626516620137340)
XLA Ops:
  0.6 111.4 %shard_map.148 = (bf16[8,2,6144]{2,1,0:T(2,128)(2,1)}, bf16[128,1024]{1,0:T(8,128)(2,1)}, bf16[128,1024]{1,0:T(8,128)(2,1)}) custom-call(s32[2,6]{1,0:T(2,128)} %bitcast.18, bf16[6,6144]{1,0:T(8,128)(2,1)} %moe_in.1, bf16[128,2,128]{2,1,0:T(2,128)(2,1)} %bitcast.15, bf16[288,6144]{1,0:T(8,128)(2,1)} %bitcast.12, bf16[288,6144]{1,0:T(8,128)(2,1)} %bitcast.13, ...), custom_call_target="tpu_custom_call" | custom-call | tf_op jit(solution)/shard_map/pallas_call | solution.py:523
  112.0 2.5 %shard_map.149 = (bf16[128,1024]{1,0:T(8,128)(2,1)}, bf16[6,6144]{1,0:T(8,128)(2,1)}, bf16[128,1024]{1,0:T(8,128)(2,1)}) custom-call(s32[2,6]{1,0:T(2,128)} %bitcast.19, f32[2,6]{1,0:T(2,128)} %bitcast.20, bf16[8,2,6144]{2,1,0:T(2,128)(2,1)} %get-tuple-element.6.ret, bf16[128,1024]{1,0:T(8,128)(2,1)} %get-tuple-element.7.lin, ...), custom_call_target="tpu_custom_call" | custom-call | tf_op jit(solution)/shard_map/pallas_call | solution.py:580
